TPU v7x, 32 devices: a whole 2x2x4 slice. The times are simulated.
32 devices in a mesh: tile: 16 (over z, y, x), chan: 2 (over core).
Axes of the slice: x: 2, y: 2, z: 4, core: 2. Of those that a mesh axis runs over, the one named last changes fastest.
Arguments:
- visibility: bfloat16 [4, 2, 131072], P('chan', None, 'tile'), may hold values from -5 to 5
- u_kernel: bfloat16 [4, 8, 131072], P('chan', None, 'tile'), may hold values from 0.099609375 to 1
- v_kernel: bfloat16 [4, 8, 131072], P('chan', None, 'tile'), may hold values from 0.099609375 to 1
- u_offset: int32 [131072], P('tile'), may hold values from 0 to 120
- v_offset: int32 [131072], P('tile'), may hold values from 0 to 120
- tile_route: int32 [512, 1], P('tile'), may hold values from 0 to 15; in each aligned block of 32 rows (0 to 31, 32 to 63, ...) at most 8 rows name the same one
- tile_slot: int32 [512], P('tile'), may hold values from 0 to 7
Outputs:
- image: float32 [1024, 1024], P(('tile', 'chan'))
Inputs may be any that keep to these rules, and one draw needn't show every extreme that they name: `tile_route`: in the 32 blocks of one device at most 8 name the same owner, a bound that some block reaches of them.
All inputs are finite; a program needn't handle non-finite values.
Results may differ from a plain program's by a relative error of at most 0.0021.
The roundings to bfloat16 on the way count: a program that leaves them out, or rounds other values in their place, can miss the bound.
Values may be sent and summed in bfloat16 or wider, within the bound.
No kernel may reach another device: no remote copies, remote signals or barrier semaphores. Data moves between devices by JAX's collectives and lax.ppermute only.
A program may use at most 64 MiB of HBM per device.

v0:
```python
import math

import jax
import jax.numpy as jnp
from jax import lax
from jax.sharding import PartitionSpec as P

NG = 16384
CH = 4
KS = 8
BLOCK = 256
TS = 128
TPD = 8
NB = 32
IMX = 1024
IMY = 1024


def phase_tables(rows_coord, cols_coord):
    phase_turns = jnp.mod(rows_coord[:, None] * cols_coord[None, :], NG)
    angles = phase_turns.astype(jnp.float32) * (2.0 * math.pi / NG)
    return (jnp.cos(angles).astype(jnp.bfloat16), jnp.sin(angles).astype(jnp.bfloat16))


def block_weights(vis_block, u_block, v_block, u_first, v_first):
    cell_index = jnp.arange(TS, dtype=jnp.int32)
    spread = jnp.arange(KS, dtype=jnp.int32)
    u_hit = u_first[None, :, None] + spread[:, None, None] == cell_index[None, None, :]
    v_hit = v_first[None, :, None] + spread[:, None, None] == cell_index[None, None, :]
    u_weight = jnp.sum(
        jnp.where(u_hit[None], u_block[:, :, :, None].astype(jnp.float32), 0.0), axis=1
    )
    v_weight = jnp.sum(
        jnp.where(v_hit[None], v_block[:, :, :, None].astype(jnp.float32), 0.0), axis=1
    )
    weighted = (
        jnp.swapaxes(vis_block, 1, 2).astype(jnp.float32)[:, :, :, None] * u_weight[:, :, None, :]
    )
    return (v_weight.astype(jnp.bfloat16), weighted.astype(jnp.bfloat16))


def grid_group(uv_grid, first_slot, arrays):
    vis_all, u_all, v_all, u_starts, v_starts, places = arrays

    def slot_cut(array):
        return lax.dynamic_slice_in_dim(array, first_slot, 8, 2)

    def row_cut(array):
        return lax.dynamic_slice_in_dim(array, first_slot, 8, 0)

    v_weight, weighted = jax.vmap(block_weights, in_axes=(2, 2, 2, 0, 0))(
        slot_cut(vis_all), slot_cut(u_all), slot_cut(v_all), row_cut(u_starts), row_cut(v_starts)
    )
    tiles = jnp.einsum("gckv,gckpu->gvpu", v_weight, weighted, preferred_element_type=jnp.float32)
    return uv_grid.at[row_cut(places)].add(tiles)


def body(visibility, u_kernel, v_kernel, u_offset, v_offset, tile_route, tile_slot):
    tile_count = lax.axis_size("tile")
    per_group = visibility.shape[0]
    local_rows = visibility.shape[2]
    capacity = 4 * NB // tile_count
    slot_count = tile_count * capacity
    owners = tile_route[:, 0]
    positions = jnp.arange(NB, dtype=jnp.int32)
    earlier = (owners[:, None] == owners[None, :]) & (positions[None, :] < positions[:, None])
    ranking = jnp.sum(earlier.astype(jnp.int32), axis=1)
    slot_index = owners * capacity + ranking

    def pack_slots(block_array):
        empty = jnp.zeros(block_array.shape[:2] + (slot_count, BLOCK), block_array.dtype)
        return empty.at[:, :, slot_index, :].set(block_array)

    marks = jnp.stack(
        [
            u_offset.reshape(NB, BLOCK),
            v_offset.reshape(NB, BLOCK),
            jnp.broadcast_to(tile_slot[:, None] + 1, (NB, BLOCK)),
        ]
    )
    marks = marks.astype(jnp.float32).astype(jnp.bfloat16)[:, None]
    received = (
        lax.all_to_all(
            pack_slots(visibility.reshape(per_group, 2, NB, BLOCK)),
            "tile",
            split_axis=2,
            concat_axis=2,
            tiled=True,
        ),
        lax.all_to_all(
            pack_slots(u_kernel.reshape(per_group, KS, NB, BLOCK)),
            "tile",
            split_axis=2,
            concat_axis=2,
            tiled=True,
        ),
        lax.all_to_all(
            pack_slots(v_kernel.reshape(per_group, KS, NB, BLOCK)),
            "tile",
            split_axis=2,
            concat_axis=2,
            tiled=True,
        ),
        lax.all_to_all(pack_slots(marks), "tile", split_axis=2, concat_axis=2, tiled=True),
    )
    vis_all, u_all, v_all, got_marks = received
    mark_ints = got_marks[:, 0].astype(jnp.int32)
    u_starts = mark_ints[0]
    v_starts = mark_ints[1]
    place_plus = mark_ints[2][:, 0]
    places = jnp.maximum(place_plus - 1, 0)
    grid_start = jnp.zeros((TPD, TS, 2, TS), jnp.float32)
    arrays = (vis_all, u_all, v_all, u_starts, v_starts, places)

    def plain_turn(turn_index, uv_grid):
        return grid_group(uv_grid, turn_index * 8, arrays)

    uv_grid = lax.fori_loop(0, slot_count // 8, plain_turn, grid_start)
    grid_rows = uv_grid.reshape(TPD * TS, 2 * TS).astype(jnp.bfloat16)
    v_coord = jnp.arange(TPD * TS, dtype=jnp.int32)
    rows_y = 128

    def columns_block(block_index):
        y_coord = block_index * rows_y + jnp.arange(rows_y, dtype=jnp.int32) - IMY // 2
        cos_v, sin_v = phase_tables(y_coord, v_coord)
        cos_part = jnp.dot(cos_v, grid_rows, preferred_element_type=jnp.float32)
        sin_part = jnp.dot(sin_v, grid_rows, preferred_element_type=jnp.float32)
        real_part = cos_part[:, :TS] - sin_part[:, TS:]
        imag_part = cos_part[:, TS:] + sin_part[:, :TS]
        return jnp.stack([real_part, imag_part], axis=1).astype(jnp.bfloat16)

    transformed = lax.map(columns_block, jnp.arange(IMY // rows_y, dtype=jnp.int32)).reshape(
        IMY, 2, TS
    )
    x_coord = jnp.arange(IMX, dtype=jnp.int32) - IMX // 2
    u_coord = lax.axis_index("tile") * TS + jnp.arange(TS, dtype=jnp.int32)
    cos_u, sin_u = phase_tables(u_coord, x_coord)
    summed = lax.psum_scatter(
        jnp.dot(transformed[:, 0], cos_u, preferred_element_type=jnp.float32)
        - jnp.dot(transformed[:, 1], sin_u, preferred_element_type=jnp.float32),
        ("tile", "chan"),
        scatter_dimension=0,
        tiled=True,
    )
    return summed / (KS * KS * math.sqrt(local_rows * tile_count * CH))


def solution(mesh):
    placed = (
        P("chan", None, "tile"),
        P("chan", None, "tile"),
        P("chan", None, "tile"),
        P("tile"),
        P("tile"),
        P("tile", None),
        P("tile"),
    )
    return jax.shard_map(
        body, mesh=mesh, in_specs=placed, out_specs=P(("tile", "chan"), None), check_vma=False
    )
```

profile of v0, /device:TPU:0, one launch (start us, length us, event | category | flops | bytes accessed | tf_op | source)
XLA Modules:
  0.0 671.0 jit_solution(8284557836455721492)
XLA Ops:
  14.5 8.3 %all-to-all-start = ((bf16[3,1,128,256]{3,0,1,2:T(4,128)(2,1)}), bf16[3,1,128,256]{3,0,1,2:T(4,128)(2,1)S(1)}, u32[]{:S(2)}, u32[]{:S(2)}) async-start(bf16[3,1,128,256]{3,0,1,2:T(4,128)(2,1)} %bitcast.14), calls=%async_computation | async-start | bytes 524288 | tf_op jit(solution)/shard_map/all_to_all | solution.py:104
  26.7 6.0 all-to-all-done
  40.2 5.2 all-to-all-done.2
  52.2 20.5 %all-to-all-done.1 = bf16[2,8,128,256]{3,1,0,2:T(8,128)(2,1)S(1)} async-done(((bf16[2,8,128,256]{3,1,0,2:T(8,128)(2,1)}), bf16[2,8,128,256]{3,1,0,2:T(8,128)(2,1)S(1)}, u32[]{:S(2)}, u32[]{:S(2)}) %all-to-all-start.1) | async-done | bytes 1048608 | tf_op jit(solution)/shard_map/all_to_all | solution.py:97
  72.7 5.9 all-to-all-start.3
  80.0 21.6 %all-to-all-done.3 = bf16[2,8,128,256]{3,1,0,2:T(8,128)(2,1)} async-done(((bf16[2,8,128,256]{3,1,0,2:T(8,128)(2,1)}), bf16[2,8,128,256]{3,1,0,2:T(8,128)(2,1)}, u32[]{:S(2)}, u32[]{:S(2)}) %all-to-all-start.3) | async-done | bytes 1048608 | tf_op jit(solution)/shard_map/all_to_all | solution.py:90
  101.8 351.6 %while.26 = (s32[]{:T(128)}, f32[8,128,2,128]{3,1,2,0:T(8,128)S(1)}, s32[128]{0:T(128)S(1)}, s32[128,256]{1,0:T(8,128)}, bf16[2,8,128,256]{3,1,0,2:T(8,128)(2,1)...) while((s32[]{:T(128)}, ...), condition=%wide.region_9.10_spmd, body=%wide.region_5.9_spmd.sunk | while | flops 290824224 | bytes 19955988 | solution.py:118
  114.0 5.1 select_reduce_fusion.5
  136.0 5.1 select_reduce_fusion.5
  157.9 5.1 select_reduce_fusion.5
  179.9 5.1 select_reduce_fusion.5
  201.9 5.1 select_reduce_fusion.5
  223.9 5.1 select_reduce_fusion.5
  245.9 5.1 select_reduce_fusion.5
  267.8 5.1 select_reduce_fusion.5
  289.8 5.1 select_reduce_fusion.5
  311.8 5.1 select_reduce_fusion.5
  333.8 5.1 select_reduce_fusion.5
  355.7 5.1 select_reduce_fusion.5
  377.7 5.1 select_reduce_fusion.5
  399.7 5.1 select_reduce_fusion.5
  443.6 5.1 select_reduce_fusion.5
  454.1 59.1 %while.27 = (s32[]{:T(128)}, bf16[8,128,2,128]{3,1,0,2:T(8,128)(2,1)}, s32[8]{0:T(128)S(1)}, bf16[1024,256]{1,0:T(8,128)(2,1)S(1)}, s32[]{:T(128)}, /*index=5*/s32[1]{0:T(128)}) while((s32[]{:T(128)}, bf16[8,128,2,128]{3,1,0,2:T(8,128)(2,1)}, s32[8]{0:T(128)S(1)}, bf16[1024,256]{1,0:T(8,128)(2,1)S(1)}, s32[]{:T(128)}, ...), condition=%wide.region_11.12_spmd.clone, body=%wide.region_10.11_spmd.clone.sunk | while | flops 138346752 | bytes 1771617 | solution.py:132
  521.1 141.4 %reduce-scatter.2.cloned.1.call-done = f32[32,1024]{1,0:T(8,128)} async-done(((f32[1024,1024]{1,0:T(8,128)}), f32[32,1024]{1,0:T(8,128)}) %reduce-scatter.2.cloned.1.call-update) | async-done | bytes 131088 | tf_op jit(solution)/shard_map/reduce_scatter | solution.py:138
  (284 shorter events, 364.6 us)
Async XLA Ops:
  14.5 18.2 %all-to-all-start = ((bf16[3,1,128,256]{3,0,1,2:T(4,128)(2,1)}), bf16[3,1,128,256]{3,0,1,2:T(4,128)(2,1)S(1)}, u32[]{:S(2)}, u32[]{:S(2)}) async-start(bf16[3,1,128,256]{3,0,1,2:T(4,128)(2,1)} %bitcast.14), calls=%async_computation | async-start | bytes 524288 | tf_op jit(solution)/shard_map/all_to_all | solution.py:104
  22.8 26.3 %copy-start.1 = (bf16[2,8,8192]{2,1,0:T(8,128)(2,1)S(1)}, bf16[2,8,8192]{2,1,0:T(8,128)(2,1)}, u32[]{:S(2)}) copy-start(bf16[2,8,8192]{2,1,0:T(8,128)(2,1)} %param.12) | copy-start | bytes 786436
  32.7 12.8 %all-to-all-start.2 = ((bf16[2,2,128,256]{3,1,0,2:T(2,128)(2,1)}), bf16[2,2,128,256]{3,1,0,2:T(2,128)(2,1)S(1)}, u32[]{:S(2)}, u32[]{:S(2)}) async-start(bf16[2,2,128,256]{3,1,0,2:T(2,128)(2,1)} %copy.46), calls=%async_computation.2 | async-start | bytes 524288 | tf_op jit(solution)/shard_map/all_to_all | solution.py:83
  45.4 27.3 %all-to-all-start.1 = ((bf16[2,8,128,256]{3,1,0,2:T(8,128)(2,1)}), bf16[2,8,128,256]{3,1,0,2:T(8,128)(2,1)S(1)}, u32[]{:S(2)}, u32[]{:S(2)}) async-start(bf16[2,8,128,256]{3,1,0,2:T(8,128)(2,1)} %copy.44), calls=%async_computation.1 | async-start | bytes 2097152 | tf_op jit(solution)/shard_map/all_to_all | solution.py:97
  72.7 28.9 %all-to-all-start.3 = ((bf16[2,8,128,256]{3,1,0,2:T(8,128)(2,1)}), bf16[2,8,128,256]{3,1,0,2:T(8,128)(2,1)}, u32[]{:S(2)}, u32[]{:S(2)}) async-start(bf16[2,8,128,256]{3,1,0,2:T(8,128)(2,1)} %copy.48), calls=%async_computation.3 | async-start | bytes 2097152 | tf_op jit(solution)/shard_map/all_to_all | solution.py:90
  78.6 584.0 %reduce-scatter.2.cloned.1.call-start = ((), (), s32[]{:S(2)}) async-start(), calls=%async_computation.5 | async-start | bytes 4325376 | tf_op jit(solution)/shard_map/reduce_scatter | solution.py:138
  513.2 3.6 copy-start
Sparse Core Ops, SparseCore 0:
  521.2 141.2 reduce-scatter.1
where the time goes:
time: 673 us; the launch traced here: 671 us
  other arithmetic  298 us (44%)
  waiting for transfers between devices  195 us (29%)
  matrix products  102 us (15%)
  local copies, waits for them, and re-layouts  33.7 us (5%)
  starting transfers between devices  21.6 us (3%)
  between operations  13.6 us (2%)
  loops' own time  6.94 us (1%)
    reduce_scatter x1, waiting for transfers between devices, body(): lax.psum_scatter(jnp.dot(transformed[:, 0], cos_u, preferred_element_type...  141 us
    reduce_sum x16, other arithmetic, block_weights(): jnp.sum(jnp.where(v_hit[None], v_block[:, :, :, None].astype(jnp.float32)...  81.9 us
    reduce_sum x16, other arithmetic, block_weights(): jnp.sum(jnp.where(u_hit[None], u_block[:, :, :, None].astype(jnp.float32)...  80.3 us
    dot_general x16, matrix products, grid_group(): jnp.einsum('gckv,gckpu->gvpu', v_weight, weighted, preferred_element_type...  50.5 us
    eq x16, other arithmetic, block_weights(): u_first[None, :, None] + spread[:, None, None] == cell_index[None, None, :]  44.5 us
    eq x16, other arithmetic, block_weights(): v_first[None, :, None] + spread[:, None, None] == cell_index[None, None, :]  44.5 us
    dot_general x8, matrix products, columns_block(): cos_part = jnp.dot(cos_v, grid_rows, preferred_element_type=jnp.float32)  21.8 us
    dot_general x8, matrix products, columns_block(): sin_part = jnp.dot(sin_v, grid_rows, preferred_element_type=jnp.float32)  21.8 us
  transfers between devices with their start and end apart: 5, of which 5 were waited for; matrix products, arithmetic and copies ran while one was open for 2% of the time, Pallas kernels for 0%

commit v1 on v0

v1 whole, which is shorter than its diff:
```python
import functools
import math

import jax
import jax.numpy as jnp
import ml_dtypes
import numpy as np
from jax import lax
from jax.experimental import pallas as pl
from jax.experimental.pallas import tpu as pltpu
from jax.sharding import PartitionSpec as P

NG = 16384
CH = 4
KS = 8
BLOCK = 256
TS = 128
TPD = 8
NB = 32
IMX = 1024
IMY = 1024
ROWS = 80


def phase_table(rows_coord, cols_coord):
    turns = np.mod(rows_coord[:, None].astype(np.int64) * cols_coord[None, :].astype(np.int64), NG)
    angles = turns.astype(np.float64) * (2.0 * math.pi / NG)
    return np.cos(angles).astype(ml_dtypes.bfloat16), np.sin(angles).astype(ml_dtypes.bfloat16)


def column_table():
    cos_v, sin_v = phase_table(np.arange(IMY) - IMY // 2, np.arange(TPD * TS))
    return np.concatenate([cos_v, sin_v], axis=1)


def image_table(bands):
    cos_u, sin_u = phase_table(np.arange(bands * TS), np.arange(IMX) - IMX // 2)
    both = np.stack([cos_u.reshape(bands, TS, IMX), (-sin_u).reshape(bands, TS, IMX)], axis=1)
    return both.reshape(bands * 2 * TS, IMX)


def pack_kernel(capacity, route, slot, u_ref, v_ref, vis_ref, uo_ref, vo_ref, out_ref, count):
    owners = out_ref.shape[0] // capacity
    out_ref[...] = jnp.zeros_like(out_ref)

    def clear(owner, _):
        count[owner] = 0
        return 0

    lax.fori_loop(0, owners, clear, 0)
    for block in range(NB):
        owner = route[block]
        rank = count[owner]
        count[owner] = rank + 1
        target = owner * capacity + rank
        place = jnp.full((1, TS), slot[block] + 1, jnp.int32).astype(jnp.float32)
        misc = []
        for half in range(2):
            lanes = slice(block * BLOCK + half * TS, block * BLOCK + half * TS + TS)
            row = block * 2 + half
            out_ref[target, 16 * half:16 * half + 16, :] = u_ref[:, lanes]
            out_ref[target, 32 + 16 * half:48 + 16 * half, :] = v_ref[:, lanes]
            misc += [
                vis_ref[0, :, lanes].astype(jnp.float32),
                vis_ref[1, :, lanes].astype(jnp.float32),
                uo_ref[row:row + 1, :].astype(jnp.float32),
                vo_ref[row:row + 1, :].astype(jnp.float32),
                place,
                jnp.zeros((1, TS), jnp.float32),
            ]
        out_ref[target, 64:80, :] = jnp.concatenate(misc, axis=0).astype(jnp.bfloat16)


def turned(kernel, first):
    for bit in (1, 2, 4):
        kernel = jnp.where((first & bit) != 0, pltpu.roll(kernel, bit, 0), kernel)
    return kernel


def spread(kernel, first_tile):
    both = jnp.concatenate([kernel, kernel], axis=0).astype(jnp.bfloat16)
    zero = jnp.zeros_like(both)
    return jnp.concatenate(
        [jnp.where(first_tile == pair * 2, both, zero) for pair in range(TS // 16)], axis=0
    )


def tile_of(first):
    sub = lax.broadcasted_iota(jnp.int32, (8, TS), 0)
    tile = lax.shift_right_logical(first + ((sub - first) & 7), 3)
    return jnp.concatenate([tile, tile - 1], axis=0).astype(jnp.float32).astype(jnp.bfloat16)


def block_tile(got_ref, index):
    v_parts, w_parts = [], []
    misc = got_ref[index, 64:80, :].astype(jnp.float32)
    for half in range(2):
        u_two = got_ref[index, 16 * half:16 * half + 16, :].astype(jnp.float32)
        v_two = got_ref[index, 32 + 16 * half:48 + 16 * half, :].astype(jnp.float32)
        own = misc[8 * half:8 * half + 8]
        u_first = jnp.broadcast_to(own[4:5], (8, TS)).astype(jnp.int32)
        v_first = jnp.broadcast_to(own[5:6], (8, TS)).astype(jnp.int32)
        u_tile, v_tile = tile_of(u_first), tile_of(v_first)
        for chan in range(2):
            v_parts.append(spread(turned(v_two[8 * chan:8 * chan + 8], v_first), v_tile))
            u_turned = turned(u_two[8 * chan:8 * chan + 8], u_first)
            w_parts.append(jnp.concatenate(
                [spread(u_turned * own[2 * chan + part:2 * chan + part + 1], u_tile) for part in range(2)],
                axis=0,
            ))
    v_all = jnp.concatenate(v_parts, axis=1)
    w_all = jnp.concatenate(w_parts, axis=1)
    return lax.dot_general(v_all, w_all, (((1,), (1,)), ((), ())), preferred_element_type=jnp.float32)


def grid_kernel(places, got_ref, table_hbm, out_ref, grid, table, order, sem):
    copy = pltpu.make_async_copy(table_hbm, table, sem)
    copy.start()
    grid[...] = jnp.zeros_like(grid)
    slots = got_ref.shape[0]

    def list_slot(index, carried):
        filled, spare = carried
        taken = places[index] > 0

        @pl.when(taken)
        def _():
            order[filled] = index

        return filled + taken.astype(jnp.int32), jnp.where(taken, spare, index)

    filled, spare = lax.fori_loop(0, slots, list_slot, (jnp.int32(0), jnp.int32(0)))
    order[filled] = spare

    def add_pair(turn, _):
        for lane in range(2):
            index = order[turn * 2 + lane]
            place = jnp.maximum(places[index] - 1, 0)
            rows = pl.ds(pl.multiple_of(place * TS, TS), TS)
            grid[rows, :] += block_tile(got_ref, index)
        return 0

    lax.fori_loop(0, (filled + 1) // 2, add_pair, 0)
    copy.wait()
    rounded = grid[...].astype(jnp.bfloat16)
    real, imag = rounded[:, :TS], rounded[:, TS:]
    both = jnp.concatenate([rounded, jnp.concatenate([-imag, real], axis=1)], axis=0)
    step = 256
    for first in range(0, IMY, step):
        out_ref[first:first + step, :] = jnp.dot(
            table[first:first + step, :], both, preferred_element_type=jnp.float32
        ).astype(jnp.bfloat16)


def image_kernel(scale, got_ref, table_ref, out_ref, total):
    turn = pl.program_id(0)

    @pl.when(turn == 0)
    def _():
        total[...] = jnp.zeros_like(total)

    rows = got_ref.shape[2]
    part = total[...]
    for band in range(got_ref.shape[0]):
        both = jnp.concatenate([got_ref[band, 0], got_ref[band, 1]], axis=0)
        part = part + jnp.dot(
            both, table_ref[band * 2 * TS:(band + 1) * 2 * TS, :], preferred_element_type=jnp.float32
        )
    total[...] = part

    @pl.when(turn == pl.num_programs(0) - 1)
    def _():
        out_ref[...] = (part[:rows] + part[rows:]) * scale


VMEM = pl.BlockSpec(memory_space=pltpu.VMEM)
SMEM = pl.BlockSpec(memory_space=pltpu.SMEM)
PARAMS = pltpu.CompilerParams(vmem_limit_bytes=48 * 1024 * 1024)


def body(visibility, u_kernel, v_kernel, u_offset, v_offset, tile_route, tile_slot):
    bands = lax.axis_size("tile")
    groups = lax.axis_size("chan")
    local_rows = visibility.shape[2]
    capacity = 4 * NB // bands
    slots = bands * capacity
    packed = pl.pallas_call(
        functools.partial(pack_kernel, capacity),
        out_shape=jax.ShapeDtypeStruct((slots, ROWS, TS), jnp.bfloat16),
        in_specs=[SMEM, SMEM, VMEM, VMEM, VMEM, VMEM, VMEM],
        out_specs=VMEM,
        scratch_shapes=[pltpu.SMEM((bands,), jnp.int32)],
        compiler_params=PARAMS,
    )(
        tile_route[:, 0],
        tile_slot,
        u_kernel.reshape(2 * KS, local_rows),
        v_kernel.reshape(2 * KS, local_rows),
        visibility,
        u_offset.reshape(NB * 2, TS),
        v_offset.reshape(NB * 2, TS),
    )
    got = lax.all_to_all(packed, "tile", split_axis=0, concat_axis=0, tiled=True)
    places = got[:, 70, 0].astype(jnp.int32)
    columns = pl.pallas_call(
        grid_kernel,
        out_shape=jax.ShapeDtypeStruct((IMY, 2 * TS), jnp.bfloat16),
        in_specs=[SMEM, VMEM, pl.BlockSpec(memory_space=pl.ANY)],
        out_specs=VMEM,
        scratch_shapes=[
            pltpu.VMEM((TPD * TS, 2 * TS), jnp.float32),
            pltpu.VMEM((IMY, 2 * TPD * TS), jnp.bfloat16),
            pltpu.SMEM((slots + 8,), jnp.int32),
            pltpu.SemaphoreType.DMA,
        ],
        compiler_params=PARAMS,
    )(places, got, jnp.asarray(column_table()))
    rows_y = IMY // (bands * groups)
    sent = lax.all_to_all(
        columns.reshape(bands * groups, rows_y, 2 * TS), ("tile", "chan"), split_axis=0, concat_axis=0, tiled=True
    )
    per_turn = 4
    scale = 1.0 / (KS * KS * math.sqrt(local_rows * bands * CH))
    return pl.pallas_call(
        functools.partial(image_kernel, scale),
        out_shape=jax.ShapeDtypeStruct((rows_y, IMX), jnp.float32),
        grid=(bands // per_turn,),
        in_specs=[
            pl.BlockSpec((per_turn, groups, rows_y, 2 * TS), lambda turn: (turn, 0, 0, 0)),
            pl.BlockSpec((per_turn * 2 * TS, IMX), lambda turn: (turn, 0)),
        ],
        out_specs=pl.BlockSpec((rows_y, IMX), lambda turn: (0, 0)),
        scratch_shapes=[pltpu.VMEM((groups * rows_y, IMX), jnp.float32)],
        compiler_params=PARAMS,
    )(sent.reshape(bands, groups, rows_y, 2 * TS), jnp.asarray(image_table(bands)))


def solution(mesh):
    placed = (
        P("chan", None, "tile"),
        P("chan", None, "tile"),
        P("chan", None, "tile"),
        P("tile"),
        P("tile"),
        P("tile", None),
        P("tile"),
    )
    return jax.shard_map(
        body, mesh=mesh, in_specs=placed, out_specs=P(("tile", "chan"), None), check_vma=False
    )
```

time: 673 us -> 125 us (0.19)
  other arithmetic: 298 us -> 2.35 us
  waiting for transfers between devices: 195 us -> 0 us
  matrix products: 102 us -> 0 us
  blocking collectives: 0 us -> 102 us
  local copies, waits for them, and re-layouts: 33.7 us -> 5.56 us
  starting transfers between devices: 21.6 us -> 0 us
  Pallas kernels: 0 us -> 15.5 us
  between operations: 13.6 us -> 0.03 us
  loops' own time: 6.94 us -> 0 us
    reduce_sum x33 -> x0, other arithmetic: 163 us -> none  [the longest x16 81.9 us: block_weights(): jnp.sum(jnp.where(v_hit[None], v_block[:, :, :, None].astype(jnp.float32)...]
    reduce_scatter x1 -> x0, waiting for transfers between devices: 141 us -> none  [body(): lax.psum_scatter(jnp.dot(transformed[:, 0], cos_u, preferred_element_type...]
    all_to_all x0 -> x2, blocking collectives: none -> 102 us  [the longest x1 68.2 us: body(): lax.all_to_all(packed, 'tile', split_axis=0, concat_axis=0, tiled=True)]
    dot_general x34 -> x0, matrix products: 102 us -> none  [the longest x16 50.5 us: grid_group(): jnp.einsum('gckv,gckpu->gvpu', v_weight, weighted, preferred_element_type...]
    eq x32 -> x0, other arithmetic: 89 us -> none  [the longest x16 44.5 us: block_weights(): u_first[None, :, None] + spread[:, None, None] == cell_index[None, None, :]]
    all_to_all x4 -> x0, waiting for transfers between devices: 53.3 us -> none  [the longest x1 21.6 us: body(): lax.all_to_all(pack_slots(u_kernel.reshape(per_group, KS, NB, BLOCK)), 't...]
    all_to_all x4 -> x0, starting transfers between devices: 21.4 us -> none  [the longest x1 8.32 us: body(): lax.all_to_all(pack_slots(marks), 'tile', split_axis=2, concat_axis=2, ti...]
    scatter-add x16 -> x0, other arithmetic: 21 us -> none  [grid_group(): return uv_grid.at[row_cut(places)].add(tiles)]
  transfers between devices with their start and end apart: 5 -> 0, of which waited for: 5 -> 0; matrix products, arithmetic and copies ran while one was open for 2% -> 0% of each run, Pallas kernels for 0% -> 0%
where the time goes in v1:
time: 125 us; the launch traced here: 126 us
  blocking collectives  102 us (82%)
  Pallas kernels  15.5 us (12%)
  local copies, waits for them, and re-layouts  5.56 us (4%)
  other arithmetic  2.35 us (2%)
    all_to_all x1, blocking collectives, body(): lax.all_to_all(packed, 'tile', split_axis=0, concat_axis=0, tiled=True)  68.2 us
    all_to_all x1, blocking collectives, body(): lax.all_to_all(columns.reshape(bands * groups, rows_y, 2 * TS), ('tile',...  34.2 us
    pallas_call x1, Pallas kernels, body(): pl.pallas_call(grid_kernel, out_shape=jax.ShapeDtypeStruct((IMY, 2 * TS),...  8.7 us
    pallas_call x1, Pallas kernels, body(): pl.pallas_call(functools.partial(image_kernel, scale), out_shape=jax.Shap...  5.62 us
    unnamed x14, local copies, waits for them, and re-layouts  5.56 us

profile of v1, /device:TPU:0, one launch (start us, length us, event | category | flops | bytes accessed | tf_op | source)
XLA Modules:
  0.0 125.8 jit_solution(3855273653665538838)
XLA Ops:
  0.0 0.0 copy-start
  0.0 0.9 copy-done
  1.0 0.0 copy-start.1
  1.0 0.9 copy-done.1
  1.9 0.0 copy-start.2
  1.9 0.8 copy-done.2
  2.7 0.0 copy-start.3
  2.7 0.8 copy-done.3
  3.5 0.0 copy-start.4
  3.5 0.8 copy-done.4
  4.3 0.0 copy-start.5
  4.3 0.7 copy-done.5
  4.9 0.0 copy-start.6
  4.9 0.7 copy-done.6
  5.6 1.2 shard_map.91
  6.8 68.2 %all_to_all.10.got_ref = bf16[128,80,128]{2,1,0:T(8,128)(2,1)S(1)} all-to-all(bf16[128,80,128]{2,1,0:T(8,128)(2,1)S(1)} %shard_map.91), channel_id=1, replica_groups=mesh['tile'=16,'chan'=2] {'tile'}, dimensions={0} | all-to-all | bytes 5242880 | tf_op jit(solution)/shard_map/all_to_all | solution.py:203
  75.0 2.4 %fusion.places = s32[128]{0:T(128)S(1)} fusion(bf16[128,80,128]{2,1,0:T(8,128)(2,1)S(1)} %all_to_all.10.got_ref), kind=kLoop, calls=%fused_computation.1 | loop fusion | flops 128 | bytes 768 | tf_op jit(solution)/shard_map/convert_element_type | solution.py:204
  77.3 8.7 %shard_map.92 = bf16[1024,256]{1,0:T(8,128)(2,1)S(1)} custom-call(s32[128]{0:T(128)S(1)} %fusion.places, bf16[128,80,128]{2,1,0:T(8,128)(2,1)S(1)} %all_to_all.10.got_ref, bf16[1024,2048]{1,0:T(8,128)(2,1)} %constant.4.clone.table_hbm), custom_call_target="tpu_custom_call" | custom-call | tf_op jit(solution)/shard_map/pallas_call | solution.py:205
  86.0 34.2 %all_to_all.11 = bf16[32,32,256]{2,1,0:T(8,128)(2,1)S(1)} all-to-all(bf16[32,32,256]{2,1,0:T(8,128)(2,1)S(1)} %bitcast.8), channel_id=1, replica_groups=mesh['tile'=16,'chan'=2] {'tile','chan'}, dimensions={0} | all-to-all | bytes 1048576 | tf_op jit(solution)/shard_map/all_to_all | solution.py:219
  120.2 5.6 %shard_map.93 = f32[32,1024]{1,0:T(8,128)} custom-call(bf16[16,2,32,256]{3,2,1,0:T(8,128)(2,1)S(1)} %bitcast.7, bf16[4096,1024]{1,0:T(8,128)(2,1)} %constant.5.clone.table_ref), custom_call_target="tpu_custom_call" | custom-call | tf_op jit(solution)/shard_map/pallas_call | solution.py:224
Async XLA Ops:
  0.0 0.9 copy-start
  1.0 0.9 copy-start.1
  1.9 0.8 copy-start.2
  2.7 0.8 copy-start.3
  3.5 0.8 copy-start.4
  4.3 0.7 copy-start.5
  4.9 0.7 copy-start.6

commit v2 on v1

v2 whole, which is shorter than its diff:
```python
import functools
import math

import jax
import jax.numpy as jnp
import ml_dtypes
import numpy as np
from jax import lax
from jax.experimental import pallas as pl
from jax.experimental.pallas import tpu as pltpu
from jax.sharding import PartitionSpec as P

NG = 16384
CH = 4
KS = 8
BLOCK = 256
TS = 128
TPD = 8
NB = 32
IMX = 1024
IMY = 1024
ROWS = 80
TILES = ROWS // 16
DIRECT = 2
MANY = 255


def phase_table(rows_coord, cols_coord):
    turns = np.mod(rows_coord[:, None].astype(np.int64) * cols_coord[None, :].astype(np.int64), NG)
    angles = turns.astype(np.float64) * (2.0 * math.pi / NG)
    return np.cos(angles).astype(ml_dtypes.bfloat16), np.sin(angles).astype(ml_dtypes.bfloat16)


def column_table():
    cos_v, sin_v = phase_table(np.arange(IMY) - IMY // 2, np.arange(TPD * TS))
    return np.concatenate([cos_v, sin_v], axis=1)


def image_table(bands):
    cos_u, sin_u = phase_table(np.arange(bands * TS), np.arange(IMX) - IMX // 2)
    both = np.stack([cos_u.reshape(bands, TS, IMX), (-sin_u).reshape(bands, TS, IMX)], axis=1)
    return both


def shared_table(both):
    bands = both.shape[0]
    cut = both.reshape(bands, 2, bands, TS // bands, IMX)
    return np.swapaxes(cut, 1, 2).reshape(bands * 2 * TS, IMX)


def full_pack_kernel(capacity, route, slot, u_ref, v_ref, vis_ref, uo_ref, vo_ref, out_ref, count):
    owners = out_ref.shape[0] // (capacity * TILES)
    out_ref[...] = jnp.zeros_like(out_ref)

    def clear(owner, _):
        count[owner] = 0
        return 0

    lax.fori_loop(0, owners, clear, 0)
    for block in range(NB):
        owner = route[block]
        rank = count[owner]
        count[owner] = rank + 1
        base = (owner * capacity + rank) * TILES
        place = jnp.full((1, TS), slot[block] + 1, jnp.int32).astype(jnp.float32)
        misc = []
        for half in range(2):
            lanes = slice(block * BLOCK + half * TS, block * BLOCK + half * TS + TS)
            row = block * 2 + half
            out_ref[base + half] = u_ref[:, lanes]
            out_ref[base + 2 + half] = v_ref[:, lanes]
            misc += [
                vis_ref[0, :, lanes].astype(jnp.float32),
                vis_ref[1, :, lanes].astype(jnp.float32),
                uo_ref[row:row + 1, :].astype(jnp.float32),
                vo_ref[row:row + 1, :].astype(jnp.float32),
                place,
                jnp.zeros((1, TS), jnp.float32),
            ]
        out_ref[base + 4] = jnp.concatenate(misc, axis=0).astype(jnp.bfloat16)


def turned(kernel, first):
    for bit in (1, 2, 4):
        kernel = jnp.where((first & bit) != 0, pltpu.roll(kernel, bit, 0), kernel)
    return kernel


def spread(kernel, first_tile):
    both = jnp.concatenate([kernel, kernel], axis=0).astype(jnp.bfloat16)
    zero = jnp.zeros_like(both)
    return jnp.concatenate(
        [jnp.where(first_tile == pair * 2, both, zero) for pair in range(TS // 16)], axis=0
    )


def tile_of(first, twice):
    sub = lax.broadcasted_iota(jnp.int32, (8, TS), 0)
    tile = lax.shift_right_logical(first + ((sub - first) & 7), 3)
    return jnp.concatenate([tile, tile if twice else tile - 1], axis=0).astype(jnp.float32).astype(jnp.bfloat16)


def spread_pair(first, second, first_tile):
    both = jnp.concatenate([first, second], axis=0).astype(jnp.bfloat16)
    zero = jnp.zeros_like(both)
    return jnp.concatenate([jnp.where(first_tile == tile, both, zero) for tile in range(TS // 8)], axis=0)


def block_factors(halves, shared):
    v_parts, w_parts = [], []
    for u_two, v_two, own in halves:
        u_first = jnp.broadcast_to(own[4:5], (8, TS)).astype(jnp.int32)
        v_first = jnp.broadcast_to(own[5:6], (8, TS)).astype(jnp.int32)
        u_tile, v_tile = tile_of(u_first, shared), tile_of(v_first, False)
        for chan in range(2):
            v_parts.append(spread(turned(v_two[8 * chan:8 * chan + 8], v_first), v_tile))
            u_turned = turned(u_two[8 * chan:8 * chan + 8], u_first)
            real, imag = [u_turned * own[2 * chan + part:2 * chan + part + 1] for part in range(2)]
            if shared:
                w_parts.append(spread_pair(real, imag, u_tile))
            else:
                w_parts.append(jnp.concatenate([spread(real, u_tile), spread(imag, u_tile)], axis=0))
    return jnp.concatenate(v_parts, axis=1), jnp.concatenate(w_parts, axis=1)


def dot_rows(left, right):
    return lax.dot_general(left, right, (((1,), (1,)), ((), ())), preferred_element_type=jnp.float32)


def pack_kernel(
    bands, shared,
    route_hbm, slot_hbm, u_hbm, v_hbm, vis_hbm, uo_hbm, vo_hbm, out_ref,
    route, slot, u_ref, v_ref, vis_ref, uo_ref, vo_ref, count, listed, grid, sems,
):
    pairs = (
        (route_hbm, route), (slot_hbm, slot), (u_hbm, u_ref), (v_hbm, v_ref),
        (vis_hbm, vis_ref), (uo_hbm, uo_ref), (vo_hbm, vo_ref),
    )
    copies = [pltpu.make_async_copy(source, target, sems.at[turn]) for turn, (source, target) in enumerate(pairs)]
    for copy in copies:
        copy.start()
    per_owner = out_ref.shape[0] // bands

    def clear(owner, _):
        count[owner] = 0
        return 0

    lax.fori_loop(0, bands, clear, 0)
    if shared:
        grid[...] = jnp.zeros_like(grid)
    copies[0].wait()
    copies[1].wait()

    mark = jnp.int32(0)
    if shared:
        for block in range(NB):
            owner = route[block]
            seen = count[owner]
            count[owner] = seen + 1
            mark = jnp.where(seen == DIRECT, jnp.where(mark == 0, owner + 1, MANY), mark)
        lax.fori_loop(0, bands, clear, 0)
    marks = jnp.broadcast_to(mark, (1, TS)).astype(jnp.float32)
    nothing = jnp.zeros((7, TS), jnp.float32)
    blank = jnp.concatenate([nothing, marks, nothing, marks], axis=0).astype(jnp.bfloat16)
    empty = jnp.zeros((16, TS), jnp.bfloat16)
    for owner in range(bands):
        for rank in range(DIRECT):
            base = owner * per_owner + rank * TILES
            for tile in range(TILES - 1):
                out_ref[base + tile] = empty
            out_ref[base + TILES - 1] = blank
    for copy in copies[2:]:
        copy.wait()

    filled = jnp.int32(0)
    for block in range(NB):
        owner = route[block]
        rank = count[owner]
        count[owner] = rank + 1
        apart = (owner + 1 == mark) | (rank >= DIRECT)
        base = owner * per_owner + rank * TILES
        if shared:
            listed[filled] = block
            filled = filled + apart.astype(jnp.int32)

        @pl.when(jnp.logical_not(apart))
        def _():
            place = jnp.full((1, TS), slot[block] + 1, jnp.int32).astype(jnp.float32)
            misc = []
            for half in range(2):
                lanes = slice(block * BLOCK + half * TS, block * BLOCK + half * TS + TS)
                row = block * 2 + half
                out_ref[base + half] = u_ref[:, lanes]
                out_ref[base + 2 + half] = v_ref[:, lanes]
                misc += [
                    vis_ref[0, :, lanes].astype(jnp.float32),
                    vis_ref[1, :, lanes].astype(jnp.float32),
                    uo_ref[row:row + 1, :].astype(jnp.float32),
                    vo_ref[row:row + 1, :].astype(jnp.float32),
                    place,
                    marks,
                ]
            out_ref[base + 4] = jnp.concatenate(misc, axis=0).astype(jnp.bfloat16)

    if not shared:
        return

    def add_block(turn, _):
        block = listed[turn]
        halves = []
        for half in range(2):
            lanes = pl.ds(pl.multiple_of(block * BLOCK + half * TS, TS), TS)
            row = pl.ds(block * 2 + half, 1)
            own = jnp.concatenate(
                [
                    vis_ref[0, :, lanes].astype(jnp.float32),
                    vis_ref[1, :, lanes].astype(jnp.float32),
                    uo_ref[row, :].astype(jnp.float32),
                    vo_ref[row, :].astype(jnp.float32),
                ],
                axis=0,
            )
            halves.append((u_ref[:, lanes].astype(jnp.float32), v_ref[:, lanes].astype(jnp.float32), own))
        v_all, w_all = block_factors(halves, True)
        cells = pl.ds(pl.multiple_of(slot[block] * TS, TS), TS)
        grid[:, cells] += dot_rows(w_all, v_all)
        return 0

    lax.fori_loop(0, filled, add_block, 0)
    for owner in range(bands):
        for place in range(TPD):
            out_ref[owner * per_owner + DIRECT * TILES + place] = grid[
                16 * owner:16 * owner + 16, TS * place:TS * place + TS
            ].astype(jnp.bfloat16)


def got_tile(got_ref, base):
    misc = got_ref[base + 4].astype(jnp.float32)
    halves = [
        (got_ref[base + half].astype(jnp.float32), got_ref[base + 2 + half].astype(jnp.float32), misc[8 * half:8 * half + 8])
        for half in range(2)
    ]
    v_all, w_all = block_factors(halves, False)
    return misc, dot_rows(v_all, w_all)


def write_columns(grid, table, out_ref, extra):
    rounded = grid[...].astype(jnp.bfloat16)
    real, imag = rounded[:, :TS], rounded[:, TS:]
    both = jnp.concatenate([rounded, jnp.concatenate([-imag, real], axis=1)], axis=0)
    rows = IMY // out_ref.shape[0]
    step = 256
    for first in range(0, IMY, step):
        part = jnp.dot(table[first:first + step, :], both, preferred_element_type=jnp.float32)
        if extra is not None:
            more = dot_rows(extra, table[first:first + step, :])
        for row in range(0, step, rows):
            pieces = [part[row:row + rows, :TS], part[row:row + rows, TS:]]
            if extra is not None:
                lane = row // TS * TS
                pieces.append(more[:, lane:lane + TS])
            elif out_ref.shape[1] > 2 * rows:
                pieces.append(jnp.zeros((out_ref.shape[1] - 2 * rows, TS), jnp.float32))
            out_ref[(first + row) // rows] = jnp.concatenate(pieces, axis=0).astype(jnp.bfloat16)


def full_grid_kernel(places, got_ref, table_hbm, out_ref, grid, table, sem):
    copy = pltpu.make_async_copy(table_hbm, table, sem)
    copy.start()
    grid[...] = jnp.zeros_like(grid)
    tiles = got_ref.shape[0]

    def add_slot(index, _):
        @pl.when(places[index] > 0)
        def _():
            rows = pl.ds(pl.multiple_of((places[index] - 1) * TS, TS), TS)
            grid[rows, :] += got_tile(got_ref, index * TILES)[1]

        return 0

    lax.fori_loop(0, tiles // TILES, add_slot, 0)
    copy.wait()
    write_columns(grid, table, out_ref, None)


def grid_kernel(bands, shared, got_ref, table_hbm, out_ref, flags, grid, table, sem):
    copy = pltpu.make_async_copy(table_hbm, table, sem)
    copy.start()
    grid[...] = jnp.zeros_like(grid)
    per_owner = got_ref.shape[0] // bands

    def add_source(source, carried):
        least, most = carried
        for rank in range(DIRECT):
            misc, tile = got_tile(got_ref, source * per_owner + rank * TILES)
            place = jnp.maximum(misc[6, 0].astype(jnp.int32) - 1, 0)
            rows = pl.ds(pl.multiple_of(place * TS, TS), TS)
            grid[rows, :] += tile
        return jnp.minimum(least, misc[:8]), jnp.maximum(most, misc[:8])

    start = (jnp.full((8, TS), float(MANY), jnp.float32), jnp.zeros((8, TS), jnp.float32))
    least, most = lax.fori_loop(0, bands, add_source, start)
    low, high = least[7, 0].astype(jnp.int32), most[7, 0].astype(jnp.int32)
    flags[0] = ((low == high) & (high != MANY)).astype(jnp.int32)
    flags[1] = jnp.maximum(jnp.where(high == MANY, 0, high) - 1, 0)
    extra = None
    if shared:
        parts = []
        for place in range(TPD):
            total = jnp.zeros((16, TS), jnp.float32)
            for source in range(bands):
                total += got_ref[source * per_owner + DIRECT * TILES + place].astype(jnp.float32)
            parts.append(total)
        own = jnp.concatenate(parts, axis=1).astype(jnp.bfloat16).astype(jnp.float32)
        other = jnp.concatenate([-own[8:], own[:8]], axis=0)
        extra = jnp.concatenate([own, other], axis=1).astype(jnp.bfloat16)
    copy.wait()
    write_columns(grid, table, out_ref, extra)


def band_dot(got_ref, table_ref, first, rows):
    total = None
    for band in range(got_ref.shape[0]):
        both = jnp.concatenate(
            [
                jnp.concatenate([got_ref[band, group, :rows, :], got_ref[band, group, rows:2 * rows, :]], axis=1)
                for group in range(got_ref.shape[1])
            ],
            axis=0,
        )
        part = jnp.dot(
            both, table_ref[band * 2 * TS:(band + 1) * 2 * TS, :], preferred_element_type=jnp.float32
        )
        total = part if total is None else total + part
    return total


def image_kernel(scale, flags, got_ref, table_ref, shared_hbm, out_ref, shared, sem):
    rows = out_ref.shape[0]
    lines = shared.shape[0]
    copy = pltpu.make_async_copy(
        shared_hbm.at[pl.ds(pl.multiple_of(flags[1] * lines, lines), lines), :], shared, sem
    )
    copy.start()
    total = band_dot(got_ref, table_ref, 0, rows)
    image = total[:rows] + total[rows:]
    turn = (lax.axis_index("tile") * got_ref.shape[1] + lax.axis_index("chan")) % (TS // rows)
    copy.wait()
    for group in range(got_ref.shape[1]):
        left = jnp.concatenate([got_ref[band, group, 2 * rows:, :] for band in range(got_ref.shape[0])], axis=0)
        left = pltpu.roll(left.astype(jnp.float32), lax.rem(TS - turn * rows, TS), 1)[:, :rows].astype(jnp.bfloat16)
        image = image + lax.dot_general(
            left, shared[...], (((0,), (0,)), ((), ())), preferred_element_type=jnp.float32
        )
    out_ref[...] = image * scale


def plain_image_kernel(scale, got_ref, table_ref, out_ref, total):
    turn = pl.program_id(0)

    @pl.when(turn == 0)
    def _():
        total[...] = jnp.zeros_like(total)

    rows = out_ref.shape[0]
    total[...] += band_dot(got_ref, table_ref, 0, rows)

    @pl.when(turn == pl.num_programs(0) - 1)
    def _():
        out_ref[...] = (total[:rows] + total[rows:]) * scale


VMEM = pl.BlockSpec(memory_space=pltpu.VMEM)
SMEM = pl.BlockSpec(memory_space=pltpu.SMEM)
ANY = pl.BlockSpec(memory_space=pl.ANY)
PARAMS = pltpu.CompilerParams(vmem_limit_bytes=40 * 1024 * 1024)


def body(visibility, u_kernel, v_kernel, u_offset, v_offset, tile_route, tile_slot):
    bands = lax.axis_size("tile")
    groups = lax.axis_size("chan")
    local_rows = visibility.shape[2]
    capacity = 4 * NB // bands
    shared = capacity > DIRECT
    per_owner = DIRECT * TILES + (TPD if shared else 0)
    rows_y = IMY // (bands * groups)
    sent_rows = 2 * rows_y + (16 if shared else 0)
    columns_shape = jax.ShapeDtypeStruct((bands * groups, sent_rows, TS), jnp.bfloat16)
    v_table = jnp.asarray(column_table())
    both = image_table(bands)
    u_table = jnp.asarray(both.reshape(bands * 2 * TS, IMX))
    operands = (
        tile_route[:, 0],
        tile_slot,
        u_kernel.reshape(2 * KS, local_rows),
        v_kernel.reshape(2 * KS, local_rows),
        visibility,
        u_offset.reshape(NB * 2, TS),
        v_offset.reshape(NB * 2, TS),
    )
    grid_scratch = [
        pltpu.VMEM((TPD * TS, 2 * TS), jnp.float32),
        pltpu.VMEM((IMY, 2 * TPD * TS), jnp.bfloat16),
        pltpu.SemaphoreType.DMA,
    ]
    packed = pl.pallas_call(
        functools.partial(pack_kernel, bands, shared),
        out_shape=jax.ShapeDtypeStruct((bands * per_owner, 16, TS), jnp.bfloat16),
        in_specs=[ANY] * 7,
        out_specs=VMEM,
        scratch_shapes=[
            pltpu.SMEM((NB,), jnp.int32),
            pltpu.SMEM((NB,), jnp.int32),
            pltpu.VMEM((2 * KS, local_rows), jnp.bfloat16),
            pltpu.VMEM((2 * KS, local_rows), jnp.bfloat16),
            pltpu.VMEM(visibility.shape, jnp.bfloat16),
            pltpu.VMEM((NB * 2, TS), jnp.int32),
            pltpu.VMEM((NB * 2, TS), jnp.int32),
            pltpu.SMEM((bands,), jnp.int32),
            pltpu.SMEM((NB + 1,), jnp.int32),
            pltpu.VMEM((2 * TS, TPD * TS), jnp.float32),
            pltpu.SemaphoreType.DMA((7,)),
        ],
        compiler_params=PARAMS,
    )(*operands)
    got = lax.all_to_all(packed, "tile", split_axis=0, concat_axis=0, tiled=True)
    columns, flags = pl.pallas_call(
        functools.partial(grid_kernel, bands, shared),
        out_shape=(columns_shape, jax.ShapeDtypeStruct((2,), jnp.int32)),
        in_specs=[VMEM, ANY],
        out_specs=(VMEM, SMEM),
        scratch_shapes=grid_scratch,
        compiler_params=PARAMS,
    )(got, v_table)

    def every_slot(_):
        slots = bands * capacity
        packed = pl.pallas_call(
            functools.partial(full_pack_kernel, capacity),
            out_shape=jax.ShapeDtypeStruct((slots * TILES, 16, TS), jnp.bfloat16),
            in_specs=[SMEM, SMEM, VMEM, VMEM, VMEM, VMEM, VMEM],
            out_specs=VMEM,
            scratch_shapes=[pltpu.SMEM((bands,), jnp.int32)],
            compiler_params=PARAMS,
        )(*operands)
        got = lax.all_to_all(packed, "tile", split_axis=0, concat_axis=0, tiled=True)
        places = got.reshape(slots, TILES, 16, TS)[:, TILES - 1, 6, 0].astype(jnp.int32)
        return pl.pallas_call(
            full_grid_kernel,
            out_shape=columns_shape,
            in_specs=[SMEM, VMEM, ANY],
            out_specs=VMEM,
            scratch_shapes=grid_scratch,
            compiler_params=PARAMS,
        )(places, got, v_table)

    if shared:
        columns = lax.cond(flags[0] == 1, lambda kept: kept, every_slot, columns)
    sent = lax.all_to_all(columns, ("tile", "chan"), split_axis=0, concat_axis=0, tiled=True)
    sent = sent.reshape(bands, groups, sent_rows, TS)
    scale = 1.0 / (KS * KS * math.sqrt(local_rows * bands * CH))
    out_shape = jax.ShapeDtypeStruct((rows_y, IMX), jnp.float32)
    if shared:
        return pl.pallas_call(
            functools.partial(image_kernel, scale),
            out_shape=out_shape,
            in_specs=[SMEM, VMEM, VMEM, ANY],
            out_specs=VMEM,
            scratch_shapes=[pltpu.VMEM((2 * TS, IMX), jnp.bfloat16), pltpu.SemaphoreType.DMA],
            compiler_params=PARAMS,
        )(flags, sent, u_table, jnp.asarray(shared_table(both)))
    per_turn = 4
    return pl.pallas_call(
        functools.partial(plain_image_kernel, scale),
        out_shape=out_shape,
        grid=(bands // per_turn,),
        in_specs=[
            pl.BlockSpec((per_turn, groups, sent_rows, TS), lambda turn: (turn, 0, 0, 0)),
            pl.BlockSpec((per_turn * 2 * TS, IMX), lambda turn: (turn, 0)),
        ],
        out_specs=pl.BlockSpec((rows_y, IMX), lambda turn: (0, 0)),
        scratch_shapes=[pltpu.VMEM((groups * rows_y, IMX), jnp.float32)],
        compiler_params=PARAMS,
    )(sent, u_table)


def solution(mesh):
    placed = (
        P("chan", None, "tile"),
        P("chan", None, "tile"),
        P("chan", None, "tile"),
        P("tile"),
        P("tile"),
        P("tile", None),
        P("tile"),
    )
    return jax.shard_map(
        body, mesh=mesh, in_specs=placed, out_specs=P(("tile", "chan"), None), check_vma=False
    )
```

time: 125 us -> 77.7 us (0.62)
  blocking collectives: 102 us -> 22.8 us
  waiting for transfers between devices: 0 us -> 26.9 us
  starting transfers between devices: 0 us -> 8.33 us
  other arithmetic: 2.35 us -> 0 us
  local copies, waits for them, and re-layouts: 5.56 us -> 3.43 us
    all_to_all x2 -> x1, blocking collectives: 102 us -> 22.8 us  [body(): lax.all_to_all(columns, ('tile', 'chan'), split_axis=0, concat_axis=0, ti...]
    all_to_all x0 -> x1, waiting for transfers between devices: none -> 26.9 us  [body(): lax.all_to_all(packed, 'tile', split_axis=0, concat_axis=0, tiled=True)]
    all_to_all x0 -> x1, starting transfers between devices: none -> 8.33 us  [body(): lax.all_to_all(packed, 'tile', split_axis=0, concat_axis=0, tiled=True)]
    convert_element_type x1 -> x0, other arithmetic: 2.35 us -> none  [body(): places = got[:, 70, 0].astype(jnp.int32)]
    unnamed x14 -> x16, local copies, waits for them, and re-layouts: 5.56 us -> 3.43 us
  transfers between devices with their start and end apart: 0 -> 1, of which waited for: 0 -> 1; matrix products, arithmetic and copies ran while one was open for 0% -> 0% of each run, Pallas kernels for 0% -> 0%
where the time goes in v2:
time: 77.7 us; the launch traced here: 77.4 us
  waiting for transfers between devices  26.9 us (35%)
  blocking collectives  22.8 us (29%)
  Pallas kernels  15.8 us (20%)
  starting transfers between devices  8.33 us (11%)
  local copies, waits for them, and re-layouts  3.43 us (4%)
    all_to_all x1, waiting for transfers between devices, body(): lax.all_to_all(packed, 'tile', split_axis=0, concat_axis=0, tiled=True)  26.9 us
    all_to_all x1, blocking collectives, body(): lax.all_to_all(columns, ('tile', 'chan'), split_axis=0, concat_axis=0, ti...  22.8 us
    all_to_all x1, starting transfers between devices, body(): lax.all_to_all(packed, 'tile', split_axis=0, concat_axis=0, tiled=True)  8.33 us
    pallas_call x1, Pallas kernels, body(): pl.pallas_call(functools.partial(grid_kernel, bands, shared), out_shape=(...  7.85 us
    pallas_call x1, Pallas kernels, body(): pl.pallas_call(functools.partial(pack_kernel, bands, shared), out_shape=j...  4.82 us
    unnamed x16, local copies, waits for them, and re-layouts  3.43 us
    pallas_call x1, Pallas kernels, body(): pl.pallas_call(functools.partial(image_kernel, scale), out_shape=out_shap...  3.08 us
  transfers between devices with their start and end apart: 1, of which 1 were waited for; matrix products, arithmetic and copies ran while one was open for 0% of the time, Pallas kernels for 0%

profile of v2, /device:TPU:0, one launch (start us, length us, event | category | flops | bytes accessed | tf_op | source)
XLA Modules:
  0.0 77.4 jit_solution(7085727608213402660)
XLA Ops:
  0.0 4.8 %shard_map.100 = bf16[288,16,128]{2,1,0:T(8,128)(2,1)} custom-call(s32[32]{0:T(128)} %bitcast.23, s32[32]{0:T(128)} %slot_hbm.1, bf16[16,8192]{1,0:T(8,128)(2,1)} %bitcast.15, bf16[16,8192]{1,0:T(8,128)(2,1)} %bitcast.17, bf16[2,2,8192]{2,1,0:T(2,128)(2,1)} %vis_hbm.1, s32[64,128]{1,0:T(8,128)} %bitcast.19, s32[64,128]{1,0:T(8,128)} %bitcast.21), custom_call_target="tpu_custom_call" | custom-call | tf_op jit(solution)/shard_map/pallas_call | solution.py:406
  4.8 8.3 %all-to-all-start.1 = ((bf16[288,16,128]{2,1,0:T(8,128)(2,1)}), bf16[288,16,128]{2,1,0:T(8,128)(2,1)S(1)}, u32[]{:S(2)}, u32[]{:S(2)}) async-start(bf16[288,16,128]{2,1,0:T(8,128)(2,1)} %shard_map.100), calls=%async_computation.1 | async-start | bytes 2359296 | tf_op jit(solution)/shard_map/all_to_all | solution.py:426
  13.2 0.0 copy-start.1
  13.2 0.0 copy-start.2
  13.2 0.0 copy-start.3
  13.2 0.0 copy-start.4
  13.2 0.0 copy-start.5
  13.2 0.0 copy-start.6
  13.2 0.0 copy-start.7
  13.3 26.9 %all-to-all-done.1.got_ref = bf16[288,16,128]{2,1,0:T(8,128)(2,1)S(1)} async-done(((bf16[288,16,128]{2,1,0:T(8,128)(2,1)}), bf16[288,16,128]{2,1,0:T(8,128)(2,1)S(1)}, u32[]{:S(2)}, u32[]{:S(2)}) %all-to-all-start.1) | async-done | bytes 1179680 | tf_op jit(solution)/shard_map/all_to_all | solution.py:426
  40.2 7.9 %shard_map.101 = (bf16[32,80,128]{2,1,0:T(8,128)(2,1)S(1)}, s32[2]{0:T(128)S(1)}) custom-call(bf16[288,16,128]{2,1,0:T(8,128)(2,1)S(1)} %all-to-all-done.1.got_ref, bf16[1024,2048]{1,0:T(8,128)(2,1)} %constant.9.clone.table_hbm), custom_call_target="tpu_custom_call" | custom-call | tf_op jit(solution)/shard_map/pallas_call | solution.py:427
  48.1 0.0 copy-done.1
  48.1 0.0 copy-done.2
  48.1 0.0 copy-done.3
  48.1 0.0 copy-done.4
  48.1 0.0 copy-done.5
  48.1 0.0 copy-done.6
  48.1 0.0 copy-done.7
  48.2 22.8 %all_to_all.15 = bf16[32,80,128]{2,1,0:T(8,128)(2,1)S(1)} all-to-all(bf16[32,80,128]{2,1,0:T(8,128)(2,1)S(1)} %get-tuple-element.37), channel_id=1, replica_groups=mesh['tile'=16,'chan'=2] {'tile','chan'}, dimensions={0} | all-to-all | bytes 1310720 | tf_op jit(solution)/shard_map/all_to_all | solution.py:459
  71.0 0.0 copy-start
  71.0 3.4 %copy-done = bf16[4096,1024]{1,0:T(8,128)(2,1)S(1)} copy-done((bf16[4096,1024]{1,0:T(8,128)(2,1)S(1)}, bf16[4096,1024]{1,0:T(8,128)(2,1)}, u32[]{:S(2)}) %copy-start) | copy-done | bytes 8388632
  74.3 3.1 %shard_map.102 = f32[32,1024]{1,0:T(8,128)} custom-call(s32[2]{0:T(128)S(1)} %get-tuple-element.35.flags, bf16[16,2,80,128]{3,2,1,0:T(8,128)(2,1)S(1)} %bitcast.13, bf16[4096,1024]{1,0:T(8,128)(2,1)S(1)} %copy-done, bf16[4096,1024]{1,0:T(8,128)(2,1)} %constant.11.clone.shared_hbm), custom_call_target="tpu_custom_call" | custom-call | tf_op jit(solution)/shard_map/pallas_call | solution.py:464
  (1 shorter events, 0.0 us)
Async XLA Ops:
  4.8 35.3 %all-to-all-start.1 = ((bf16[288,16,128]{2,1,0:T(8,128)(2,1)}), bf16[288,16,128]{2,1,0:T(8,128)(2,1)S(1)}, u32[]{:S(2)}, u32[]{:S(2)}) async-start(bf16[288,16,128]{2,1,0:T(8,128)(2,1)} %shard_map.100), calls=%async_computation.1 | async-start | bytes 2359296 | tf_op jit(solution)/shard_map/all_to_all | solution.py:426
  13.2 34.9 %copy-start.1 = (bf16[2,8,8192]{2,1,0:T(8,128)(2,1)S(1)}, bf16[2,8,8192]{2,1,0:T(8,128)(2,1)}, u32[]{:S(2)}) copy-start(bf16[2,8,8192]{2,1,0:T(8,128)(2,1)} %param.13) | copy-start | bytes 786436
  13.2 34.9 %copy-start.2 = (bf16[2,8,8192]{2,1,0:T(8,128)(2,1)S(1)}, bf16[2,8,8192]{2,1,0:T(8,128)(2,1)}, u32[]{:S(2)}) copy-start(bf16[2,8,8192]{2,1,0:T(8,128)(2,1)} %param.14) | copy-start | bytes 786436
  13.2 34.9 %copy-start.3 = (bf16[2,2,8192]{2,1,0:T(2,128)(2,1)S(1)}, bf16[2,2,8192]{2,1,0:T(2,128)(2,1)}, u32[]{:S(2)}) copy-start(bf16[2,2,8192]{2,1,0:T(2,128)(2,1)} %vis_hbm.1) | copy-start | bytes 196612
  13.2 34.9 %copy-start.4 = (s32[8192]{0:T(1024)S(1)}, s32[8192]{0:T(1024)}, u32[]{:S(2)}) copy-start(s32[8192]{0:T(1024)} %param.15) | copy-start | bytes 98308
  13.2 34.9 %copy-start.5 = (s32[8192]{0:T(1024)S(1)}, s32[8192]{0:T(1024)}, u32[]{:S(2)}) copy-start(s32[8192]{0:T(1024)} %param.16) | copy-start | bytes 98308
  13.2 34.9 %copy-start.6 = (s32[32,1]{0,1:T(1,128)S(1)}, s32[32,1]{0,1:T(1,128)}, u32[]{:S(2)}) copy-start(s32[32,1]{0,1:T(1,128)} %param.17) | copy-start | bytes 388
  13.2 34.9 %copy-start.7 = (s32[32]{0:T(128)S(1)}, s32[32]{0:T(128)}, u32[]{:S(2)}) copy-start(s32[32]{0:T(128)} %slot_hbm.1) | copy-start | bytes 388
  71.0 3.4 %copy-start = (bf16[4096,1024]{1,0:T(8,128)(2,1)S(1)}, bf16[4096,1024]{1,0:T(8,128)(2,1)}, u32[]{:S(2)}) copy-start(bf16[4096,1024]{1,0:T(8,128)(2,1)} %constant.10.clone.table_ref) | copy-start | bytes 25165828

commit v3 on v2

v3 whole, which is shorter than its diff:
```python
import functools
import math

import jax
import jax.numpy as jnp
import ml_dtypes
import numpy as np
from jax import lax
from jax.experimental import pallas as pl
from jax.experimental.pallas import tpu as pltpu
from jax.sharding import PartitionSpec as P

NG = 16384
CH = 4
KS = 8
BLOCK = 256
TS = 128
TPD = 8
NB = 32
IMX = 1024
IMY = 1024
ROWS = 80
TILES = ROWS // 16
DIRECT = 2
PEERS = 4
MANY = 255


def phase_table(rows_coord, cols_coord):
    turns = np.mod(rows_coord[:, None].astype(np.int64) * cols_coord[None, :].astype(np.int64), NG)
    angles = turns.astype(np.float64) * (2.0 * math.pi / NG)
    return np.cos(angles).astype(ml_dtypes.bfloat16), np.sin(angles).astype(ml_dtypes.bfloat16)


def column_table():
    cos_v, sin_v = phase_table(np.arange(IMY) - IMY // 2, np.arange(TPD * TS))
    return np.concatenate([cos_v, sin_v], axis=1)


def image_table(bands):
    cos_u, sin_u = phase_table(np.arange(bands * TS), np.arange(IMX) - IMX // 2)
    both = np.stack([cos_u.reshape(bands, TS, IMX), (-sin_u).reshape(bands, TS, IMX)], axis=1)
    return both.reshape(bands * 2 * TS, IMX)


def full_pack_kernel(capacity, route, slot, u_ref, v_ref, vis_ref, uo_ref, vo_ref, out_ref, count):
    owners = out_ref.shape[0] // (capacity * TILES)
    out_ref[...] = jnp.zeros_like(out_ref)

    def clear(owner, _):
        count[owner] = 0
        return 0

    lax.fori_loop(0, owners, clear, 0)
    for block in range(NB):
        owner = route[block]
        rank = count[owner]
        count[owner] = rank + 1
        base = (owner * capacity + rank) * TILES
        place = jnp.full((1, TS), slot[block] + 1, jnp.int32).astype(jnp.float32)
        misc = []
        for half in range(2):
            lanes = slice(block * BLOCK + half * TS, block * BLOCK + half * TS + TS)
            row = block * 2 + half
            out_ref[base + half] = u_ref[:, lanes]
            out_ref[base + 2 + half] = v_ref[:, lanes]
            misc += [
                vis_ref[0, :, lanes].astype(jnp.float32),
                vis_ref[1, :, lanes].astype(jnp.float32),
                uo_ref[row:row + 1, :].astype(jnp.float32),
                vo_ref[row:row + 1, :].astype(jnp.float32),
                place,
                jnp.zeros((1, TS), jnp.float32),
            ]
        out_ref[base + 4] = jnp.concatenate(misc, axis=0).astype(jnp.bfloat16)


def turned(kernel, first):
    for bit in (1, 2, 4):
        kernel = jnp.where((first & bit) != 0, pltpu.roll(kernel, bit, 0), kernel)
    return kernel


def spread(kernel, first_tile):
    both = jnp.concatenate([kernel, kernel], axis=0).astype(jnp.bfloat16)
    zero = jnp.zeros_like(both)
    return jnp.concatenate(
        [jnp.where(first_tile == pair * 2, both, zero) for pair in range(TS // 16)], axis=0
    )


def tile_of(first):
    sub = lax.broadcasted_iota(jnp.int32, (8, TS), 0)
    tile = lax.shift_right_logical(first + ((sub - first) & 7), 3)
    return jnp.concatenate([tile, tile - 1], axis=0).astype(jnp.float32).astype(jnp.bfloat16)


def block_tile(halves):
    v_parts, w_parts = [], []
    for u_two, v_two, own in halves:
        u_first = jnp.broadcast_to(own[4:5], (8, TS)).astype(jnp.int32)
        v_first = jnp.broadcast_to(own[5:6], (8, TS)).astype(jnp.int32)
        u_tile, v_tile = tile_of(u_first), tile_of(v_first)
        for chan in range(2):
            v_parts.append(spread(turned(v_two[8 * chan:8 * chan + 8], v_first), v_tile))
            u_turned = turned(u_two[8 * chan:8 * chan + 8], u_first)
            w_parts.append(jnp.concatenate(
                [spread(u_turned * own[2 * chan + part:2 * chan + part + 1], u_tile) for part in range(2)],
                axis=0,
            ))
    return dot_rows(jnp.concatenate(w_parts, axis=1), jnp.concatenate(v_parts, axis=1))


def dot_rows(left, right):
    return lax.dot_general(left, right, (((1,), (1,)), ((), ())), preferred_element_type=jnp.float32)


def start_all(pairs, sems):
    copies = [pltpu.make_async_copy(source, target, sems.at[turn]) for turn, (source, target) in enumerate(pairs)]
    for copy in copies:
        copy.start()
    return copies


def clear_counts(count, bands):
    def clear(owner, _):
        count[owner] = 0
        return 0

    lax.fori_loop(0, bands, clear, 0)


def overflow_mark(route, count):
    mark = jnp.int32(0)
    for block in range(NB):
        owner = route[block]
        seen = count[owner]
        count[owner] = seen + 1
        mark = jnp.where(seen == DIRECT, jnp.where(mark == 0, owner + 1, MANY), mark)
    return mark


def pack_kernel(
    bands, shared,
    route_hbm, slot_hbm, u_hbm, v_hbm, vis_hbm, uo_hbm, vo_hbm, out_ref,
    route, slot, u_ref, v_ref, vis_ref, uo_ref, vo_ref, count, sems,
):
    copies = start_all(
        (
            (route_hbm, route), (slot_hbm, slot), (u_hbm, u_ref), (v_hbm, v_ref),
            (vis_hbm, vis_ref), (uo_hbm, uo_ref), (vo_hbm, vo_ref),
        ),
        sems,
    )
    per_owner = DIRECT * TILES
    clear_counts(count, bands)
    copies[0].wait()
    copies[1].wait()
    mark = jnp.int32(0)
    if shared:
        mark = overflow_mark(route, count)
        clear_counts(count, bands)
    marks = jnp.broadcast_to(mark, (1, TS)).astype(jnp.float32)
    nothing = jnp.zeros((7, TS), jnp.float32)
    blank = jnp.concatenate([nothing, marks, nothing, marks], axis=0).astype(jnp.bfloat16)
    empty = jnp.zeros((16, TS), jnp.bfloat16)
    for target in range(bands * DIRECT):
        for tile in range(TILES - 1):
            out_ref[target * TILES + tile] = empty
        out_ref[target * TILES + TILES - 1] = blank
    for copy in copies[2:]:
        copy.wait()

    for block in range(NB):
        owner = route[block]
        rank = count[owner]
        count[owner] = rank + 1
        base = owner * per_owner + rank * TILES

        @pl.when((owner + 1 != mark) & (rank < DIRECT))
        def _():
            place = jnp.full((1, TS), slot[block] + 1, jnp.int32).astype(jnp.float32)
            misc = []
            for half in range(2):
                lanes = slice(block * BLOCK + half * TS, block * BLOCK + half * TS + TS)
                row = block * 2 + half
                out_ref[base + half] = u_ref[:, lanes]
                out_ref[base + 2 + half] = v_ref[:, lanes]
                misc += [
                    vis_ref[0, :, lanes].astype(jnp.float32),
                    vis_ref[1, :, lanes].astype(jnp.float32),
                    uo_ref[row:row + 1, :].astype(jnp.float32),
                    vo_ref[row:row + 1, :].astype(jnp.float32),
                    place,
                    marks,
                ]
            out_ref[base + 4] = jnp.concatenate(misc, axis=0).astype(jnp.bfloat16)


def own_kernel(
    bands,
    route_hbm, slot_hbm, u_hbm, v_hbm, vis_hbm, uo_hbm, vo_hbm, out_0, out_1, out_2, out_3,
    route, slot, u_ref, v_ref, vis_ref, uo_ref, vo_ref, count, listed, grid, sems,
):
    copies = start_all(
        (
            (route_hbm, route), (slot_hbm, slot), (u_hbm, u_ref), (v_hbm, v_ref), (vis_hbm, vis_ref),
            (uo_hbm, uo_ref), (vo_hbm, vo_ref),
        ),
        sems,
    )
    grid[...] = jnp.zeros_like(grid)
    clear_counts(count, bands)
    copies[0].wait()
    copies[1].wait()
    mark = overflow_mark(route, count)
    filled = jnp.int32(0)
    for block in range(NB):
        listed[filled] = block
        filled = filled + (route[block] + 1 == mark).astype(jnp.int32)
    for copy in copies[2:]:
        copy.wait()

    def add_block(turn, _):
        block = listed[turn]
        halves = []
        for half in range(2):
            lanes = pl.ds(pl.multiple_of(block * BLOCK + half * TS, TS), TS)
            row = pl.ds(block * 2 + half, 1)
            own = jnp.concatenate(
                [
                    vis_ref[0, :, lanes].astype(jnp.float32),
                    vis_ref[1, :, lanes].astype(jnp.float32),
                    uo_ref[row, :].astype(jnp.float32),
                    vo_ref[row, :].astype(jnp.float32),
                ],
                axis=0,
            )
            halves.append((u_ref[:, lanes].astype(jnp.float32), v_ref[:, lanes].astype(jnp.float32), own))
        cells = pl.ds(pl.multiple_of(slot[block] * TS, TS), TS)
        grid[:, cells] += block_tile(halves)
        return 0

    lax.fori_loop(0, filled, add_block, 0)
    me = lax.axis_index("tile") % PEERS
    width = TS // PEERS
    for turn, out_ref in enumerate((out_0, out_1, out_2, out_3)):
        first = pl.multiple_of((me ^ turn) * width, width)
        for part in range(2):
            out_ref[part * width:(part + 1) * width, :] = grid[pl.ds(part * TS + first, width), :].astype(jnp.bfloat16)


def own_columns_kernel(got_0, got_1, got_2, got_3, table_hbm, out_ref, table, sem):
    copy = pltpu.make_async_copy(table_hbm, table, sem)
    copy.start()
    total = got_0[...].astype(jnp.float32)
    for got_ref in (got_1, got_2, got_3):
        total += got_ref[...].astype(jnp.float32)
    both = turned_parts(total.astype(jnp.bfloat16))
    rows = IMY // out_ref.shape[0]
    step = 256
    copy.wait()
    for first in range(0, IMY, step):
        part = dot_rows(table[first:first + step, :], both)
        for row in range(0, step, rows):
            pieces = [part[row:row + rows // 2], part[row + rows // 2:row + rows]]
            out_ref[(first + row) // rows] = jnp.concatenate(pieces, axis=1).astype(jnp.bfloat16)


def got_tile(got_ref, base):
    misc = got_ref[base + 4].astype(jnp.float32)
    halves = [
        (got_ref[base + half].astype(jnp.float32), got_ref[base + 2 + half].astype(jnp.float32), misc[8 * half:8 * half + 8])
        for half in range(2)
    ]
    return misc, block_tile(halves)


def turned_parts(rounded):
    half = rounded.shape[0] // 2
    return jnp.concatenate([rounded, jnp.concatenate([-rounded[half:], rounded[:half]], axis=0)], axis=1)


def write_columns(grid, table, out_ref):
    both = turned_parts(grid[...].astype(jnp.bfloat16))
    rows = IMY // out_ref.shape[0]
    step = 256
    for first in range(0, IMY, step):
        part = dot_rows(table[first:first + step, :], both)
        for row in range(0, step, rows):
            pieces = [part[row:row + rows, :TS], part[row:row + rows, TS:]]
            out_ref[(first + row) // rows, :2 * rows, :] = jnp.concatenate(pieces, axis=0).astype(jnp.bfloat16)


def full_grid_kernel(places, got_ref, table_hbm, out_ref, grid, table, sem):
    copy = pltpu.make_async_copy(table_hbm, table, sem)
    copy.start()
    grid[...] = jnp.zeros_like(grid)
    tiles = got_ref.shape[0]

    def add_slot(index, _):
        @pl.when(places[index] > 0)
        def _():
            cells = pl.ds(pl.multiple_of((places[index] - 1) * TS, TS), TS)
            grid[:, cells] += got_tile(got_ref, index * TILES)[1]

        return 0

    lax.fori_loop(0, tiles // TILES, add_slot, 0)
    out_ref[...] = jnp.zeros_like(out_ref)
    copy.wait()
    write_columns(grid, table, out_ref)


def grid_kernel(bands, shared, got_ref, *refs):
    if shared:
        partial, table_hbm, out_ref, flags, grid, table, sem = refs
    else:
        table_hbm, out_ref, flags, grid, table, sem = refs
    copy = pltpu.make_async_copy(table_hbm, table, sem)
    copy.start()
    grid[...] = jnp.zeros_like(grid)
    per_owner = DIRECT * TILES

    def add_source(source, carried):
        least, most = carried
        for rank in range(DIRECT):
            misc, tile = got_tile(got_ref, source * per_owner + rank * TILES)
            place = jnp.maximum(misc[6, 0].astype(jnp.int32) - 1, 0)
            cells = pl.ds(pl.multiple_of(place * TS, TS), TS)
            grid[:, cells] += tile
        marks = misc[:8]
        return jnp.minimum(least, jnp.where(marks == 0.0, float(MANY), marks)), jnp.maximum(most, marks)

    start = (jnp.full((8, TS), float(MANY), jnp.float32), jnp.zeros((8, TS), jnp.float32))
    least, most = lax.fori_loop(0, bands, add_source, start, unroll=4)
    low, high = least[7, 0].astype(jnp.int32), most[7, 0].astype(jnp.int32)
    flags[0] = ((high == 0) | ((low == high) & (high != MANY))).astype(jnp.int32)
    flags[1] = jnp.where(high == MANY, 0, jnp.maximum(high - 1, 0))
    if shared:
        out_ref[:, out_ref.shape[1] - 16:, :] = partial[...]
    copy.wait()
    write_columns(grid, table, out_ref)


def side_by_side(got_ref, band, group, first, rows):
    return jnp.concatenate(
        [got_ref[band, group, first:first + rows, :], got_ref[band, group, first + rows:first + 2 * rows, :]], axis=1
    )


def band_dot(got_ref, table_ref, rows, copies=()):
    total = None
    for band in range(got_ref.shape[0]):
        both = jnp.concatenate([side_by_side(got_ref, band, group, 0, rows) for group in range(got_ref.shape[1])], axis=0)
        if copies:
            copies[band].wait()
        part = jnp.dot(
            both, table_ref[band * 2 * TS:(band + 1) * 2 * TS, :], preferred_element_type=jnp.float32
        )
        total = part if total is None else total + part
    return total


def image_kernel(scale, flags, got_ref, table_hbm, out_ref, table_ref, total, sems):
    rows = out_ref.shape[0]
    bands, groups = got_ref.shape[:2]
    pairs = []
    for band in range(bands):
        lines = pl.ds(band * 2 * TS, 2 * TS)
        pairs.append((table_hbm.at[lines, :], table_ref.at[lines, :]))
    total[...] = band_dot(got_ref, table_ref, rows, start_all(pairs, sems))
    width = TS // PEERS
    left, right = [], []
    for peer in range(PEERS):
        per_group = []
        for group in range(groups):
            added = got_ref[peer, group, 2 * rows:, :].astype(jnp.float32)
            for band in range(peer + PEERS, bands, PEERS):
                added += got_ref[band, group, 2 * rows:, :].astype(jnp.float32)
            per_group += [added[:, :2 * width], added[:, 2 * width:]]
        left.append(jnp.concatenate(per_group, axis=0))
        for part in range(2):
            first = pl.multiple_of((flags[1] * 2 + part) * TS + peer * width, width)
            right.append(table_ref[pl.ds(first, width), :])
    total[...] += jnp.dot(
        jnp.concatenate(left, axis=1).astype(jnp.bfloat16),
        jnp.concatenate(right, axis=0),
        preferred_element_type=jnp.float32,
    )
    image = total[:rows]
    for group in range(1, groups):
        image = image + total[group * rows:(group + 1) * rows]
    out_ref[...] = image * scale


def plain_image_kernel(scale, got_ref, table_ref, out_ref, total):
    turn = pl.program_id(0)

    @pl.when(turn == 0)
    def _():
        total[...] = jnp.zeros_like(total)

    rows = out_ref.shape[0]
    total[...] += band_dot(got_ref, table_ref, rows)

    @pl.when(turn == pl.num_programs(0) - 1)
    def _():
        out_ref[...] = (total[:rows] + total[rows:]) * scale


VMEM = pl.BlockSpec(memory_space=pltpu.VMEM)
SMEM = pl.BlockSpec(memory_space=pltpu.SMEM)
HBM = pl.BlockSpec(memory_space=pltpu.HBM)
PARAMS = pltpu.CompilerParams(vmem_limit_bytes=20 * 1024 * 1024)


def body(visibility, u_kernel, v_kernel, u_offset, v_offset, tile_route, tile_slot):
    bands = lax.axis_size("tile")
    groups = lax.axis_size("chan")
    local_rows = visibility.shape[2]
    capacity = 4 * NB // bands
    shared = capacity > DIRECT
    rows_y = IMY // (bands * groups)
    sent_rows = 2 * rows_y + (16 if shared else 0)
    columns_shape = jax.ShapeDtypeStruct((bands * groups, sent_rows, TS), jnp.bfloat16)
    v_table = jnp.asarray(column_table())
    operands = (
        tile_route[:, 0],
        tile_slot,
        u_kernel.reshape(2 * KS, local_rows),
        v_kernel.reshape(2 * KS, local_rows),
        visibility,
        u_offset.reshape(NB * 2, TS),
        v_offset.reshape(NB * 2, TS),
    )
    grid_scratch = [
        pltpu.VMEM((2 * TS, TPD * TS), jnp.float32),
        pltpu.VMEM((IMY, 2 * TPD * TS), jnp.bfloat16),
        pltpu.SemaphoreType.DMA,
    ]
    raw_scratch = [
        pltpu.SMEM((NB,), jnp.int32),
        pltpu.SMEM((NB,), jnp.int32),
        pltpu.VMEM((2 * KS, local_rows), jnp.bfloat16),
        pltpu.VMEM((2 * KS, local_rows), jnp.bfloat16),
        pltpu.VMEM(visibility.shape, jnp.bfloat16),
        pltpu.VMEM((NB * 2, TS), jnp.int32),
        pltpu.VMEM((NB * 2, TS), jnp.int32),
    ]
    packed = pl.pallas_call(
        functools.partial(pack_kernel, bands, shared),
        out_shape=jax.ShapeDtypeStruct((bands * DIRECT * TILES, 16, TS), jnp.bfloat16),
        in_specs=[HBM] * 7,
        out_specs=VMEM,
        scratch_shapes=raw_scratch + [pltpu.SMEM((bands,), jnp.int32), pltpu.SemaphoreType.DMA((7,))],
        compiler_params=PARAMS,
    )(*operands)
    got = lax.all_to_all(packed, "tile", split_axis=0, concat_axis=0, tiled=True)
    partial = ()
    if shared:
        own = pl.pallas_call(
            functools.partial(own_kernel, bands),
            out_shape=[jax.ShapeDtypeStruct((2 * TS // PEERS, TPD * TS), jnp.bfloat16)] * PEERS,
            in_specs=[HBM] * 7,
            out_specs=[VMEM] * PEERS,
            scratch_shapes=raw_scratch + [
                pltpu.SMEM((bands,), jnp.int32),
                pltpu.SMEM((NB + 1,), jnp.int32),
                pltpu.VMEM((2 * TS, TPD * TS), jnp.float32),
                pltpu.SemaphoreType.DMA((7,)),
            ],
            compiler_params=PARAMS,
            cost_estimate=pl.CostEstimate(flops=10 ** 9, bytes_accessed=2 * 10 ** 6, transcendentals=0),
        )(*operands)
        summed = [own[0]] + [
            lax.ppermute(own[turn], "tile", [(band, band ^ turn) for band in range(bands)]) for turn in range(1, PEERS)
        ]
        partial = (
            pl.pallas_call(
                own_columns_kernel,
                out_shape=jax.ShapeDtypeStruct((bands * groups, 16, TS), jnp.bfloat16),
                in_specs=[VMEM] * PEERS + [HBM],
                out_specs=VMEM,
                scratch_shapes=[pltpu.VMEM((IMY, 2 * TPD * TS), jnp.bfloat16), pltpu.SemaphoreType.DMA],
                compiler_params=PARAMS,
                cost_estimate=pl.CostEstimate(flops=10 ** 9, bytes_accessed=5 * 10 ** 6, transcendentals=0),
            )(*summed, v_table),
        )
    columns, flags = pl.pallas_call(
        functools.partial(grid_kernel, bands, shared),
        out_shape=(columns_shape, jax.ShapeDtypeStruct((2,), jnp.int32)),
        in_specs=[VMEM] * (1 + len(partial)) + [HBM],
        out_specs=(VMEM, SMEM),
        scratch_shapes=grid_scratch,
        compiler_params=PARAMS,
    )(got, *partial, v_table)

    def every_slot(_):
        slots = bands * capacity
        packed = pl.pallas_call(
            functools.partial(full_pack_kernel, capacity),
            out_shape=jax.ShapeDtypeStruct((slots * TILES, 16, TS), jnp.bfloat16),
            in_specs=[SMEM, SMEM, VMEM, VMEM, VMEM, VMEM, VMEM],
            out_specs=VMEM,
            scratch_shapes=[pltpu.SMEM((bands,), jnp.int32)],
            compiler_params=PARAMS,
        )(*operands)
        got = lax.all_to_all(packed, "tile", split_axis=0, concat_axis=0, tiled=True)
        places = got.reshape(slots, TILES, 16, TS)[:, TILES - 1, 6, 0].astype(jnp.int32)
        return pl.pallas_call(
            full_grid_kernel,
            out_shape=columns_shape,
            in_specs=[SMEM, VMEM, HBM],
            out_specs=VMEM,
            scratch_shapes=grid_scratch,
            compiler_params=PARAMS,
        )(places, got, v_table)

    if shared:
        columns = lax.cond(flags[0] == 1, lambda kept: kept, every_slot, columns)
    sent = lax.all_to_all(columns, ("tile", "chan"), split_axis=0, concat_axis=0, tiled=True)
    sent = sent.reshape(bands, groups, sent_rows, TS)
    scale = 1.0 / (KS * KS * math.sqrt(local_rows * bands * CH))
    out_shape = jax.ShapeDtypeStruct((rows_y, IMX), jnp.float32)
    if shared:
        u_table = jnp.asarray(np.pad(image_table(bands), ((0, 2048), (0, 0))))
        return pl.pallas_call(
            functools.partial(image_kernel, scale),
            out_shape=out_shape,
            in_specs=[SMEM, VMEM, HBM],
            out_specs=VMEM,
            scratch_shapes=[
                pltpu.VMEM((bands * 2 * TS, IMX), jnp.bfloat16),
                pltpu.VMEM((groups * rows_y, IMX), jnp.float32),
                pltpu.SemaphoreType.DMA((bands,)),
            ],
            compiler_params=pltpu.CompilerParams(vmem_limit_bytes=52 * 1024 * 1024),
        )(flags, sent, u_table)
    per_turn = 4
    return pl.pallas_call(
        functools.partial(plain_image_kernel, scale),
        out_shape=out_shape,
        grid=(bands // per_turn,),
        in_specs=[
            pl.BlockSpec((per_turn, groups, sent_rows, TS), lambda turn: (turn, 0, 0, 0)),
            pl.BlockSpec((per_turn * 2 * TS, IMX), lambda turn: (turn, 0)),
        ],
        out_specs=pl.BlockSpec((rows_y, IMX), lambda turn: (0, 0)),
        scratch_shapes=[pltpu.VMEM((groups * rows_y, IMX), jnp.float32)],
        compiler_params=PARAMS,
    )(sent, jnp.asarray(image_table(bands)))


def solution(mesh):
    placed = (
        P("chan", None, "tile"),
        P("chan", None, "tile"),
        P("chan", None, "tile"),
        P("tile"),
        P("tile"),
        P("tile", None),
        P("tile"),
    )
    return jax.shard_map(
        body, mesh=mesh, in_specs=placed, out_specs=P(("tile", "chan"), None), check_vma=False
    )
```

time: 77.7 us -> 63.6 us (0.82)
  waiting for transfers between devices: 26.9 us -> 9.69 us
  starting transfers between devices: 8.33 us -> 11.9 us
  local copies, waits for them, and re-layouts: 3.43 us -> 0.03 us
  Pallas kernels: 15.8 us -> 18.8 us
    all_to_all x1, waiting for transfers between devices: 26.9 us -> 0.01 us  [body(): lax.all_to_all(packed, 'tile', split_axis=0, concat_axis=0, tiled=True)]
    ppermute x0 -> x3, waiting for transfers between devices: none -> 9.69 us  [body(): lax.ppermute(own[turn], 'tile', [(band, band ^ turn) for band in range(ba...]
    pallas_call x0 -> x2, Pallas kernels: none -> 6.74 us  [the longest x1 3.55 us: body(): pl.pallas_call(own_columns_kernel, out_shape=jax.ShapeDtypeStruct((bands...]
    ppermute x0 -> x3, starting transfers between devices: none -> 3.55 us  [body(): lax.ppermute(own[turn], 'tile', [(band, band ^ turn) for band in range(ba...]
    unnamed x16 -> x14, local copies, waits for them, and re-layouts: 3.43 us -> 0.03 us
    pallas_call x1, Pallas kernels: 7.85 us -> 4.58 us  [body(): pl.pallas_call(functools.partial(grid_kernel, bands, shared), out_shape=(...]
    pallas_call x1, Pallas kernels: 4.82 us -> 2.5 us  [body(): pl.pallas_call(functools.partial(pack_kernel, bands, shared), out_shape=j...]
    pallas_call x1, Pallas kernels: 3.08 us -> 5.03 us  [body(): pl.pallas_call(functools.partial(image_kernel, scale), out_shape=out_shap...]
  transfers between devices with their start and end apart: 1 -> 4, of which waited for: 1 -> 3; matrix products, arithmetic and copies ran while one was open for 0% -> 0% of each run, Pallas kernels for 0% -> 11%
where the time goes in v3:
time: 63.6 us; the launch traced here: 63.4 us
  blocking collectives  22.7 us (36%)
  Pallas kernels  18.8 us (30%)
  starting transfers between devices  11.9 us (19%)
  waiting for transfers between devices  9.69 us (15%)
    all_to_all x1, blocking collectives, body(): lax.all_to_all(columns, ('tile', 'chan'), split_axis=0, concat_axis=0, ti...  22.7 us
    ppermute x3, waiting for transfers between devices, body(): lax.ppermute(own[turn], 'tile', [(band, band ^ turn) for band in range(ba...  9.69 us
    all_to_all x1, starting transfers between devices, body(): lax.all_to_all(packed, 'tile', split_axis=0, concat_axis=0, tiled=True)  8.32 us
    pallas_call x1, Pallas kernels, body(): pl.pallas_call(functools.partial(image_kernel, scale), out_shape=out_shap...  5.03 us
    pallas_call x1, Pallas kernels, body(): pl.pallas_call(functools.partial(grid_kernel, bands, shared), out_shape=(...  4.58 us
    pallas_call x1, Pallas kernels, body(): pl.pallas_call(own_columns_kernel, out_shape=jax.ShapeDtypeStruct((bands...  3.55 us
    ppermute x3, starting transfers between devices, body(): lax.ppermute(own[turn], 'tile', [(band, band ^ turn) for band in range(ba...  3.55 us
    pallas_call x1, Pallas kernels, body(): pl.pallas_call(functools.partial(own_kernel, bands), out_shape=[jax.Shape...  3.19 us
  transfers between devices with their start and end apart: 4, of which 3 were waited for; matrix products, arithmetic and copies ran while one was open for 0% of the time, Pallas kernels for 11%

profile of v3, /device:TPU:0, one launch (start us, length us, event | category | flops | bytes accessed | tf_op | source)
XLA Modules:
  0.0 63.4 jit_solution(8648261225318361178)
XLA Ops:
  0.0 2.5 %shard_map.91 = bf16[160,16,128]{2,1,0:T(8,128)(2,1)} custom-call(s32[32]{0:T(128)} %bitcast.27, s32[32]{0:T(128)} %slot_hbm.3, bf16[16,8192]{1,0:T(8,128)(2,1)} %bitcast.15, bf16[16,8192]{1,0:T(8,128)(2,1)} %bitcast.18, bf16[2,2,8192]{2,1,0:T(2,128)(2,1)} %vis_hbm.3, s32[64,128]{1,0:T(8,128)} %bitcast.21, s32[64,128]{1,0:T(8,128)} %bitcast.24), custom_call_target="tpu_custom_call" | custom-call | tf_op jit(solution)/shard_map/pallas_call | solution.py:451
  2.5 8.3 %all-to-all-start.1 = ((bf16[160,16,128]{2,1,0:T(8,128)(2,1)}), bf16[160,16,128]{2,1,0:T(8,128)(2,1)S(1)}, u32[]{:S(2)}, u32[]{:S(2)}) async-start(bf16[160,16,128]{2,1,0:T(8,128)(2,1)} %shard_map.91), calls=%async_computation.1 | async-start | bytes 1310720 | tf_op jit(solution)/shard_map/all_to_all | solution.py:459
  10.8 3.2 %shard_map.92 = (bf16[64,1024]{1,0:T(8,128)(2,1)S(1)}, bf16[64,1024]{1,0:T(8,128)(2,1)S(1)}, bf16[64,1024]{1,0:T(8,128)(2,1)S(1)}, bf16[64,1024]{1,0:T(8,128)(2,1)S(1)}) custom-call(s32[32]{0:T(128)} %bitcast.28, s32[32]{0:T(128)} %slot_hbm.3, bf16[16,8192]{1,0:T(8,128)(2,1)} %bitcast.16, bf16[16,8192]{1,0:T(8,128)(2,1)} %bitcast.19, ...), custom_call_target="tpu_custom_call" | custom-call | flops 1000000000 | bytes 2000000 | tf_op jit(solution)/shard_map/pallas_call | solution.py:462
  14.0 2.0 %collective-permute-start = (bf16[64,1024]{1,0:T(8,128)(2,1)S(1)}, bf16[64,1024]{1,0:T(8,128)(2,1)S(1)}, u32[]{:S(2)}, u32[]{:S(2)}) collective-permute-start(bf16[64,1024]{1,0:T(8,128)(2,1)S(1)} %get-tuple-element.40), channel_id=1, source_target_pairs={{0,2},{2,0},{4,6},{6,4},{8,10},{10,8},{12,14},{14,12},{16,18},{18,... | collective-permute-start | bytes 393224 | tf_op jit(solution)/shard_map/ppermute | solution.py:477
  16.0 1.5 %collective-permute-start.1 = (bf16[64,1024]{1,0:T(8,128)(2,1)S(1)}, bf16[64,1024]{1,0:T(8,128)(2,1)S(1)}, u32[]{:S(2)}, u32[]{:S(2)}) collective-permute-start(bf16[64,1024]{1,0:T(8,128)(2,1)S(1)} %get-tuple-element.41), channel_id=1, source_target_pairs={{0,4},{2,6},{4,0},{6,2},{8,12},{10,14},{12,8},{14,10},{16,20},{18,... | collective-permute-start | bytes 393224 | tf_op jit(solution)/shard_map/ppermute | solution.py:477
  17.5 0.1 collective-permute-start.2
  17.6 5.7 %collective-permute-done.got_1 = bf16[64,1024]{1,0:T(8,128)(2,1)S(1)} collective-permute-done((bf16[64,1024]{1,0:T(8,128)(2,1)S(1)}, bf16[64,1024]{1,0:T(8,128)(2,1)S(1)}, u32[]{:S(2)}, u32[]{:S(2)}) %collective-permute-start) | collective-permute-done | bytes 131104 | tf_op jit(solution)/shard_map/ppermute | solution.py:477
  23.3 2.2 %collective-permute-done.1.got_2 = bf16[64,1024]{1,0:T(8,128)(2,1)S(1)} collective-permute-done((bf16[64,1024]{1,0:T(8,128)(2,1)S(1)}, bf16[64,1024]{1,0:T(8,128)(2,1)S(1)}, u32[]{:S(2)}, u32[]{:S(2)}) %collective-permute-start.1) | collective-permute-done | bytes 131104 | tf_op jit(solution)/shard_map/ppermute | solution.py:477
  25.4 1.8 %collective-permute-done.2.got_3 = bf16[64,1024]{1,0:T(8,128)(2,1)S(1)} collective-permute-done((bf16[64,1024]{1,0:T(8,128)(2,1)S(1)}, bf16[64,1024]{1,0:T(8,128)(2,1)S(1)}, u32[]{:S(2)}, u32[]{:S(2)}) %collective-permute-start.2) | collective-permute-done | bytes 131104 | tf_op jit(solution)/shard_map/ppermute | solution.py:477
  27.3 0.0 copy-start.4
  27.3 0.0 copy-start.5
  27.3 0.0 copy-start.6
  27.3 3.6 %shard_map.93.refs_0_ = bf16[32,16,128]{2,1,0:T(8,128)(2,1)S(1)} custom-call(bf16[64,1024]{1,0:T(8,128)(2,1)S(1)} %get-tuple-element.39.got_0, bf16[64,1024]{1,0:T(8,128)(2,1)S(1)} %collective-permute-done.got_1, bf16[64,1024]{1,0:T(8,128)(2,1)S(1)} %collective-permute-done.1.got_2, bf16[64,1024]{1,0:T(8,128)(2,1)S(1)} %collective-permute-done.2.got_3, ...), custom_call_target="tpu_custom_call" | custom-call | flops 1000000000 | bytes 5000000 | tf_op jit(solution)/shard_map/pallas_call | solution.py:480
  30.9 0.0 all-to-all-done.1.got_ref
  30.9 4.6 %shard_map.94 = (bf16[32,80,128]{2,1,0:T(8,128)(2,1)S(1)}, s32[2]{0:T(128)S(1)}) custom-call(bf16[160,16,128]{2,1,0:T(8,128)(2,1)S(1)} %all-to-all-done.1.got_ref, bf16[32,16,128]{2,1,0:T(8,128)(2,1)S(1)} %shard_map.93.refs_0_, bf16[1024,2048]{1,0:T(8,128)(2,1)} %constant.7.clone.table_hbm.refs_1_), custom_call_target="tpu_custom_call" | custom-call | tf_op jit(solution)/shard_map/pallas_call | solution.py:490
  35.5 0.0 copy-done
  35.5 0.0 copy-done.1
  35.5 0.0 copy-done.2
  35.5 0.0 copy-done.3
  35.6 0.0 copy-done.4
  35.6 0.0 copy-done.5
  35.6 0.0 copy-done.6
  35.6 22.7 %all_to_all.15 = bf16[32,80,128]{2,1,0:T(8,128)(2,1)S(1)} all-to-all(bf16[32,80,128]{2,1,0:T(8,128)(2,1)S(1)} %get-tuple-element.45), channel_id=1, replica_groups=mesh['tile'=16,'chan'=2] {'tile','chan'}, dimensions={0} | all-to-all | bytes 1310720 | tf_op jit(solution)/shard_map/all_to_all | solution.py:522
  58.3 5.0 %shard_map.95 = f32[32,1024]{1,0:T(8,128)} custom-call(s32[2]{0:T(128)S(1)} %get-tuple-element.43.flags, bf16[16,2,80,128]{3,2,1,0:T(8,128)(2,1)S(1)} %bitcast.13, bf16[6144,1024]{1,0:T(8,128)(2,1)} %constant.8.clone.table_hbm), custom_call_target="tpu_custom_call" | custom-call | tf_op jit(solution)/shard_map/pallas_call | solution.py:528
  (5 shorter events, 0.0 us)
Async XLA Ops:
  2.5 28.4 %all-to-all-start.1 = ((bf16[160,16,128]{2,1,0:T(8,128)(2,1)}), bf16[160,16,128]{2,1,0:T(8,128)(2,1)S(1)}, u32[]{:S(2)}, u32[]{:S(2)}) async-start(bf16[160,16,128]{2,1,0:T(8,128)(2,1)} %shard_map.91), calls=%async_computation.1 | async-start | bytes 1310720 | tf_op jit(solution)/shard_map/all_to_all | solution.py:459
  14.0 9.3 %collective-permute-start = (bf16[64,1024]{1,0:T(8,128)(2,1)S(1)}, bf16[64,1024]{1,0:T(8,128)(2,1)S(1)}, u32[]{:S(2)}, u32[]{:S(2)}) collective-permute-start(bf16[64,1024]{1,0:T(8,128)(2,1)S(1)} %get-tuple-element.40), channel_id=1, source_target_pairs={{0,2},{2,0},{4,6},{6,4},{8,10},{10,8},{12,14},{14,12},{16,18},{18,... | collective-permute-start | bytes 393224 | tf_op jit(solution)/shard_map/ppermute | solution.py:477
  16.0 9.4 %collective-permute-start.1 = (bf16[64,1024]{1,0:T(8,128)(2,1)S(1)}, bf16[64,1024]{1,0:T(8,128)(2,1)S(1)}, u32[]{:S(2)}, u32[]{:S(2)}) collective-permute-start(bf16[64,1024]{1,0:T(8,128)(2,1)S(1)} %get-tuple-element.41), channel_id=1, source_target_pairs={{0,4},{2,6},{4,0},{6,2},{8,12},{10,14},{12,8},{14,10},{16,20},{18,... | collective-permute-start | bytes 393224 | tf_op jit(solution)/shard_map/ppermute | solution.py:477
  17.5 9.8 %collective-permute-start.2 = (bf16[64,1024]{1,0:T(8,128)(2,1)S(1)}, bf16[64,1024]{1,0:T(8,128)(2,1)S(1)}, u32[]{:S(2)}, u32[]{:S(2)}) collective-permute-start(bf16[64,1024]{1,0:T(8,128)(2,1)S(1)} %get-tuple-element.42), channel_id=1, source_target_pairs={{0,6},{2,4},{4,2},{6,0},{8,14},{10,12},{12,10},{14,8},{16,22},{18,... | collective-permute-start | bytes 393224 | tf_op jit(solution)/shard_map/ppermute | solution.py:477
  27.3 8.2 %copy-start = (bf16[2,8,8192]{2,1,0:T(8,128)(2,1)S(1)}, bf16[2,8,8192]{2,1,0:T(8,128)(2,1)}, u32[]{:S(2)}) copy-start(bf16[2,8,8192]{2,1,0:T(8,128)(2,1)} %param.12) | copy-start | bytes 786436
  27.3 8.3 %copy-start.1 = (bf16[2,8,8192]{2,1,0:T(8,128)(2,1)S(1)}, bf16[2,8,8192]{2,1,0:T(8,128)(2,1)}, u32[]{:S(2)}) copy-start(bf16[2,8,8192]{2,1,0:T(8,128)(2,1)} %param.13) | copy-start | bytes 786436
  27.3 8.3 %copy-start.2 = (bf16[2,2,8192]{2,1,0:T(2,128)(2,1)S(1)}, bf16[2,2,8192]{2,1,0:T(2,128)(2,1)}, u32[]{:S(2)}) copy-start(bf16[2,2,8192]{2,1,0:T(2,128)(2,1)} %vis_hbm.3) | copy-start | bytes 196612
  27.3 8.3 %copy-start.3 = (s32[8192]{0:T(1024)S(1)}, s32[8192]{0:T(1024)}, u32[]{:S(2)}) copy-start(s32[8192]{0:T(1024)} %param.14) | copy-start | bytes 98308
  27.3 8.3 %copy-start.4 = (s32[8192]{0:T(1024)S(1)}, s32[8192]{0:T(1024)}, u32[]{:S(2)}) copy-start(s32[8192]{0:T(1024)} %param.15) | copy-start | bytes 98308
  27.3 8.3 %copy-start.5 = (s32[32,1]{0,1:T(1,128)S(1)}, s32[32,1]{0,1:T(1,128)}, u32[]{:S(2)}) copy-start(s32[32,1]{0,1:T(1,128)} %param.16) | copy-start | bytes 388
  27.3 8.3 %copy-start.6 = (s32[32]{0:T(128)S(1)}, s32[32]{0:T(128)}, u32[]{:S(2)}) copy-start(s32[32]{0:T(128)} %slot_hbm.3) | copy-start | bytes 388

commit v4 on v3

--- a/solution.py
+++ b/solution.py
@@ -22,6 +22,7 @@
 ROWS = 80
 TILES = ROWS // 16
 DIRECT = 2
+HELD = 4
 PEERS = 4
 MANY = 255
 
@@ -199,13 +200,13 @@
 
 def own_kernel(
     bands,
-    route_hbm, slot_hbm, u_hbm, v_hbm, vis_hbm, uo_hbm, vo_hbm, out_0, out_1, out_2, out_3,
-    route, slot, u_ref, v_ref, vis_ref, uo_ref, vo_ref, count, listed, grid, sems,
+    route_hbm, slot_hbm, u_hbm, v_hbm, vis_hbm, uo_hbm, vo_hbm, share_0, share_1, share_2, share_3,
+    route, slot, u_ref, v_ref, vis_ref, uo_ref, vo_ref, count, sems, listed, grid,
 ):
     copies = start_all(
         (
-            (route_hbm, route), (slot_hbm, slot), (u_hbm, u_ref), (v_hbm, v_ref), (vis_hbm, vis_ref),
-            (uo_hbm, uo_ref), (vo_hbm, vo_ref),
+            (route_hbm, route), (slot_hbm, slot), (u_hbm, u_ref), (v_hbm, v_ref),
+            (vis_hbm, vis_ref), (uo_hbm, uo_ref), (vo_hbm, vo_ref),
         ),
         sems,
     )
@@ -221,50 +222,51 @@
     for copy in copies[2:]:
         copy.wait()
 
-    def add_block(turn, _):
-        block = listed[turn]
+    def own_tile(block, used):
         halves = []
         for half in range(2):
             lanes = pl.ds(pl.multiple_of(block * BLOCK + half * TS, TS), TS)
             row = pl.ds(block * 2 + half, 1)
             own = jnp.concatenate(
                 [
-                    vis_ref[0, :, lanes].astype(jnp.float32),
-                    vis_ref[1, :, lanes].astype(jnp.float32),
+                    vis_ref[0, :, lanes].astype(jnp.float32) * used,
+                    vis_ref[1, :, lanes].astype(jnp.float32) * used,
                     uo_ref[row, :].astype(jnp.float32),
                     vo_ref[row, :].astype(jnp.float32),
                 ],
                 axis=0,
             )
             halves.append((u_ref[:, lanes].astype(jnp.float32), v_ref[:, lanes].astype(jnp.float32), own))
-        cells = pl.ds(pl.multiple_of(slot[block] * TS, TS), TS)
-        grid[:, cells] += block_tile(halves)
+        return block_tile(halves)
+
+    def add_blocks(turn, _):
+        for lane in range(4):
+            number = turn * 4 + lane
+            block = listed[jnp.minimum(number, filled - 1)]
+            cells = pl.ds(pl.multiple_of(slot[block] * TS, TS), TS)
+            grid[:, cells] += own_tile(block, (number < filled).astype(jnp.float32))
         return 0
 
-    lax.fori_loop(0, filled, add_block, 0)
+    lax.fori_loop(0, (filled + 3) // 4, add_blocks, 0)
     me = lax.axis_index("tile") % PEERS
     width = TS // PEERS
-    for turn, out_ref in enumerate((out_0, out_1, out_2, out_3)):
+    for turn, share_ref in enumerate((share_0, share_1, share_2, share_3)):
         first = pl.multiple_of((me ^ turn) * width, width)
         for part in range(2):
-            out_ref[part * width:(part + 1) * width, :] = grid[pl.ds(part * TS + first, width), :].astype(jnp.bfloat16)
-
-
-def own_columns_kernel(got_0, got_1, got_2, got_3, table_hbm, out_ref, table, sem):
-    copy = pltpu.make_async_copy(table_hbm, table, sem)
-    copy.start()
-    total = got_0[...].astype(jnp.float32)
-    for got_ref in (got_1, got_2, got_3):
-        total += got_ref[...].astype(jnp.float32)
-    both = turned_parts(total.astype(jnp.bfloat16))
-    rows = IMY // out_ref.shape[0]
-    step = 256
-    copy.wait()
-    for first in range(0, IMY, step):
-        part = dot_rows(table[first:first + step, :], both)
-        for row in range(0, step, rows):
-            pieces = [part[row:row + rows // 2], part[row + rows // 2:row + rows]]
-            out_ref[(first + row) // rows] = jnp.concatenate(pieces, axis=1).astype(jnp.bfloat16)
+            share_ref[part * width:(part + 1) * width, :] = grid[pl.ds(part * TS + first, width), :].astype(jnp.bfloat16)
+
+
+def hold_kernel(flags, table_hbm, *refs):
+    parts, own, sems = refs[:-2], refs[-2], refs[-1]
+    rows = parts[0].shape[0]
+    pairs = [(table_hbm.at[pl.ds(turn * rows, rows), :], part) for turn, part in enumerate(parts)]
+    width = TS // PEERS
+    for turn in range(2 * PEERS):
+        peer, part = turn // 2, turn % 2
+        first = pl.multiple_of((flags[1] * 2 + part) * TS + peer * width, width)
+        pairs.append((table_hbm.at[pl.ds(first, width), :], own.at[pl.ds(turn * width, width), :]))
+    for copy in start_all(pairs, sems):
+        copy.wait()
 
 
 def got_tile(got_ref, base):
@@ -281,15 +283,22 @@
     return jnp.concatenate([rounded, jnp.concatenate([-rounded[half:], rounded[:half]], axis=0)], axis=1)
 
 
-def write_columns(grid, table, out_ref):
+def write_columns(grid, table, out_ref, own=None):
     both = turned_parts(grid[...].astype(jnp.bfloat16))
+    if own is not None:
+        both = jnp.concatenate([both, turned_parts(own)], axis=0)
     rows = IMY // out_ref.shape[0]
     step = 256
     for first in range(0, IMY, step):
         part = dot_rows(table[first:first + step, :], both)
         for row in range(0, step, rows):
-            pieces = [part[row:row + rows, :TS], part[row:row + rows, TS:]]
-            out_ref[(first + row) // rows, :2 * rows, :] = jnp.concatenate(pieces, axis=0).astype(jnp.bfloat16)
+            pieces = [part[row:row + rows, :TS], part[row:row + rows, TS:2 * TS]]
+            if own is not None:
+                middle = row + rows // 2
+                pieces.append(jnp.concatenate([part[row:middle, 2 * TS:], part[middle:row + rows, 2 * TS:]], axis=1))
+            out_ref[(first + row) // rows, :rows * 2 + (16 if own is not None else 0), :] = jnp.concatenate(
+                pieces, axis=0
+            ).astype(jnp.bfloat16)
 
 
 def full_grid_kernel(places, got_ref, table_hbm, out_ref, grid, table, sem):
@@ -313,10 +322,8 @@
 
 
 def grid_kernel(bands, shared, got_ref, *refs):
-    if shared:
-        partial, table_hbm, out_ref, flags, grid, table, sem = refs
-    else:
-        table_hbm, out_ref, flags, grid, table, sem = refs
+    shares = refs[:PEERS] if shared else ()
+    table_hbm, out_ref, flags, grid, table, sem = refs[len(shares):]
     copy = pltpu.make_async_copy(table_hbm, table, sem)
     copy.start()
     grid[...] = jnp.zeros_like(grid)
@@ -337,10 +344,14 @@
     low, high = least[7, 0].astype(jnp.int32), most[7, 0].astype(jnp.int32)
     flags[0] = ((high == 0) | ((low == high) & (high != MANY))).astype(jnp.int32)
     flags[1] = jnp.where(high == MANY, 0, jnp.maximum(high - 1, 0))
+    own = None
     if shared:
-        out_ref[:, out_ref.shape[1] - 16:, :] = partial[...]
+        own = shares[0][...].astype(jnp.float32)
+        for share in shares[1:]:
+            own += share[...].astype(jnp.float32)
+        own = own.astype(jnp.bfloat16)
     copy.wait()
-    write_columns(grid, table, out_ref)
+    write_columns(grid, table, out_ref, own)
 
 
 def side_by_side(got_ref, band, group, first, rows):
@@ -349,29 +360,29 @@
     )
 
 
-def band_dot(got_ref, table_ref, rows, copies=()):
-    total = None
-    for band in range(got_ref.shape[0]):
-        both = jnp.concatenate([side_by_side(got_ref, band, group, 0, rows) for group in range(got_ref.shape[1])], axis=0)
-        if copies:
-            copies[band].wait()
-        part = jnp.dot(
-            both, table_ref[band * 2 * TS:(band + 1) * 2 * TS, :], preferred_element_type=jnp.float32
-        )
-        total = part if total is None else total + part
-    return total
-
-
-def image_kernel(scale, flags, got_ref, table_hbm, out_ref, table_ref, total, sems):
+def band_dot(got_ref, table, rows, bands):
+    left = jnp.concatenate(
+        [
+            jnp.concatenate([side_by_side(got_ref, band, group, 0, rows) for band in bands], axis=1)
+            for group in range(got_ref.shape[1])
+        ],
+        axis=0,
+    )
+    return jnp.dot(left, table, preferred_element_type=jnp.float32)
+
+
+def image_kernel(scale, got_ref, *refs):
+    held = refs[:HELD]
+    own_ref, table_hbm, out_ref, table_ref, sems = refs[HELD:]
     rows = out_ref.shape[0]
     bands, groups = got_ref.shape[:2]
     pairs = []
-    for band in range(bands):
+    for band in range(HELD, bands):
         lines = pl.ds(band * 2 * TS, 2 * TS)
-        pairs.append((table_hbm.at[lines, :], table_ref.at[lines, :]))
-    total[...] = band_dot(got_ref, table_ref, rows, start_all(pairs, sems))
+        pairs.append((table_hbm.at[lines, :], table_ref.at[pl.ds((band - HELD) * 2 * TS, 2 * TS), :]))
+    copies = start_all(pairs, sems)
     width = TS // PEERS
-    left, right = [], []
+    left = []
     for peer in range(PEERS):
         per_group = []
         for group in range(groups):
@@ -380,14 +391,16 @@
                 added += got_ref[band, group, 2 * rows:, :].astype(jnp.float32)
             per_group += [added[:, :2 * width], added[:, 2 * width:]]
         left.append(jnp.concatenate(per_group, axis=0))
-        for part in range(2):
-            first = pl.multiple_of((flags[1] * 2 + part) * TS + peer * width, width)
-            right.append(table_ref[pl.ds(first, width), :])
-    total[...] += jnp.dot(
-        jnp.concatenate(left, axis=1).astype(jnp.bfloat16),
-        jnp.concatenate(right, axis=0),
-        preferred_element_type=jnp.float32,
-    )
+    total = jnp.dot(
+        jnp.concatenate(left, axis=1).astype(jnp.bfloat16), own_ref[...], preferred_element_type=jnp.float32
+    )
+    table = jnp.concatenate([part[...] for part in held], axis=0)
+    total = total + band_dot(got_ref, table, rows, range(HELD))
+    for first in range(HELD, bands, HELD):
+        for band in range(first, first + HELD):
+            copies[band - HELD].wait()
+        table = table_ref[(first - HELD) * 2 * TS:first * 2 * TS, :]
+        total = total + band_dot(got_ref, table, rows, range(first, first + HELD))
     image = total[:rows]
     for group in range(1, groups):
         image = image + total[group * rows:(group + 1) * rows]
@@ -402,11 +415,12 @@
         total[...] = jnp.zeros_like(total)
 
     rows = out_ref.shape[0]
-    total[...] += band_dot(got_ref, table_ref, rows)
+    part = total[...] + band_dot(got_ref, table_ref[...], rows, range(got_ref.shape[0]))
+    total[...] = part
 
     @pl.when(turn == pl.num_programs(0) - 1)
     def _():
-        out_ref[...] = (total[:rows] + total[rows:]) * scale
+        out_ref[...] = (part[:rows] + part[rows:]) * scale
 
 
 VMEM = pl.BlockSpec(memory_space=pltpu.VMEM)
@@ -448,15 +462,17 @@
         pltpu.VMEM((NB * 2, TS), jnp.int32),
         pltpu.VMEM((NB * 2, TS), jnp.int32),
     ]
+    raw_scratch += [pltpu.SMEM((bands,), jnp.int32), pltpu.SemaphoreType.DMA((7,))]
     packed = pl.pallas_call(
         functools.partial(pack_kernel, bands, shared),
         out_shape=jax.ShapeDtypeStruct((bands * DIRECT * TILES, 16, TS), jnp.bfloat16),
         in_specs=[HBM] * 7,
         out_specs=VMEM,
-        scratch_shapes=raw_scratch + [pltpu.SMEM((bands,), jnp.int32), pltpu.SemaphoreType.DMA((7,))],
+        scratch_shapes=raw_scratch,
         compiler_params=PARAMS,
     )(*operands)
     got = lax.all_to_all(packed, "tile", split_axis=0, concat_axis=0, tiled=True)
+    u_table = jnp.asarray(image_table(bands))
     partial = ()
     if shared:
         own = pl.pallas_call(
@@ -465,10 +481,7 @@
             in_specs=[HBM] * 7,
             out_specs=[VMEM] * PEERS,
             scratch_shapes=raw_scratch + [
-                pltpu.SMEM((bands,), jnp.int32),
-                pltpu.SMEM((NB + 1,), jnp.int32),
-                pltpu.VMEM((2 * TS, TPD * TS), jnp.float32),
-                pltpu.SemaphoreType.DMA((7,)),
+                pltpu.SMEM((NB + 1,), jnp.int32), pltpu.VMEM((2 * TS, TPD * TS), jnp.float32)
             ],
             compiler_params=PARAMS,
             cost_estimate=pl.CostEstimate(flops=10 ** 9, bytes_accessed=2 * 10 ** 6, transcendentals=0),
@@ -476,17 +489,7 @@
         summed = [own[0]] + [
             lax.ppermute(own[turn], "tile", [(band, band ^ turn) for band in range(bands)]) for turn in range(1, PEERS)
         ]
-        partial = (
-            pl.pallas_call(
-                own_columns_kernel,
-                out_shape=jax.ShapeDtypeStruct((bands * groups, 16, TS), jnp.bfloat16),
-                in_specs=[VMEM] * PEERS + [HBM],
-                out_specs=VMEM,
-                scratch_shapes=[pltpu.VMEM((IMY, 2 * TPD * TS), jnp.bfloat16), pltpu.SemaphoreType.DMA],
-                compiler_params=PARAMS,
-                cost_estimate=pl.CostEstimate(flops=10 ** 9, bytes_accessed=5 * 10 ** 6, transcendentals=0),
-            )(*summed, v_table),
-        )
+        partial = tuple(summed)
     columns, flags = pl.pallas_call(
         functools.partial(grid_kernel, bands, shared),
         out_shape=(columns_shape, jax.ShapeDtypeStruct((2,), jnp.int32)),
@@ -495,6 +498,31 @@
         scratch_shapes=grid_scratch,
         compiler_params=PARAMS,
     )(got, *partial, v_table)
+
+    scale = 1.0 / (KS * KS * math.sqrt(local_rows * bands * CH))
+    image_shape = jax.ShapeDtypeStruct((rows_y, IMX), jnp.float32)
+
+    def exchanged(columns):
+        sent = lax.all_to_all(columns, ("tile", "chan"), split_axis=0, concat_axis=0, tiled=True)
+        return sent.reshape(bands, groups, sent_rows, TS)
+
+    def plain_image(columns):
+        per_turn = 4
+        return pl.pallas_call(
+            functools.partial(plain_image_kernel, scale),
+            out_shape=image_shape,
+            grid=(bands // per_turn,),
+            in_specs=[
+                pl.BlockSpec((per_turn, groups, sent_rows, TS), lambda turn: (turn, 0, 0, 0)),
+                pl.BlockSpec((per_turn * 2 * TS, IMX), lambda turn: (turn, 0)),
+            ],
+            out_specs=pl.BlockSpec((rows_y, IMX), lambda turn: (0, 0)),
+            scratch_shapes=[pltpu.VMEM((groups * rows_y, IMX), jnp.float32)],
+            compiler_params=PARAMS,
+        )(exchanged(columns), u_table)
+
+    if not shared:
+        return plain_image(columns)
 
     def every_slot(_):
         slots = bands * capacity
@@ -508,7 +536,7 @@
         )(*operands)
         got = lax.all_to_all(packed, "tile", split_axis=0, concat_axis=0, tiled=True)
         places = got.reshape(slots, TILES, 16, TS)[:, TILES - 1, 6, 0].astype(jnp.int32)
-        return pl.pallas_call(
+        columns = pl.pallas_call(
             full_grid_kernel,
             out_shape=columns_shape,
             in_specs=[SMEM, VMEM, HBM],
@@ -516,40 +544,30 @@
             scratch_shapes=grid_scratch,
             compiler_params=PARAMS,
         )(places, got, v_table)
-
-    if shared:
-        columns = lax.cond(flags[0] == 1, lambda kept: kept, every_slot, columns)
-    sent = lax.all_to_all(columns, ("tile", "chan"), split_axis=0, concat_axis=0, tiled=True)
-    sent = sent.reshape(bands, groups, sent_rows, TS)
-    scale = 1.0 / (KS * KS * math.sqrt(local_rows * bands * CH))
-    out_shape = jax.ShapeDtypeStruct((rows_y, IMX), jnp.float32)
-    if shared:
-        u_table = jnp.asarray(np.pad(image_table(bands), ((0, 2048), (0, 0))))
-        return pl.pallas_call(
-            functools.partial(image_kernel, scale),
-            out_shape=out_shape,
-            in_specs=[SMEM, VMEM, HBM],
-            out_specs=VMEM,
-            scratch_shapes=[
-                pltpu.VMEM((bands * 2 * TS, IMX), jnp.bfloat16),
-                pltpu.VMEM((groups * rows_y, IMX), jnp.float32),
-                pltpu.SemaphoreType.DMA((bands,)),
-            ],
-            compiler_params=pltpu.CompilerParams(vmem_limit_bytes=52 * 1024 * 1024),
-        )(flags, sent, u_table)
-    per_turn = 4
-    return pl.pallas_call(
-        functools.partial(plain_image_kernel, scale),
-        out_shape=out_shape,
-        grid=(bands // per_turn,),
-        in_specs=[
-            pl.BlockSpec((per_turn, groups, sent_rows, TS), lambda turn: (turn, 0, 0, 0)),
-            pl.BlockSpec((per_turn * 2 * TS, IMX), lambda turn: (turn, 0)),
+        return plain_image(columns)
+
+    held = pl.pallas_call(
+        hold_kernel,
+        out_shape=[jax.ShapeDtypeStruct((2 * TS, IMX), jnp.bfloat16)] * HELD
+        + [jax.ShapeDtypeStruct((2 * TS, IMX), jnp.bfloat16)],
+        in_specs=[SMEM, HBM],
+        out_specs=[VMEM] * (HELD + 1),
+        scratch_shapes=[pltpu.SemaphoreType.DMA((HELD + 2 * PEERS,))],
+        compiler_params=PARAMS,
+        cost_estimate=pl.CostEstimate(flops=0, bytes_accessed=16 * 10 ** 6, transcendentals=0),
+    )(flags, u_table)
+    image = pl.pallas_call(
+        functools.partial(image_kernel, scale),
+        out_shape=image_shape,
+        in_specs=[VMEM] * (HELD + 2) + [HBM],
+        out_specs=VMEM,
+        scratch_shapes=[
+            pltpu.VMEM(((bands - HELD) * 2 * TS, IMX), jnp.bfloat16),
+            pltpu.SemaphoreType.DMA((bands - HELD,)),
         ],
-        out_specs=pl.BlockSpec((rows_y, IMX), lambda turn: (0, 0)),
-        scratch_shapes=[pltpu.VMEM((groups * rows_y, IMX), jnp.float32)],
         compiler_params=PARAMS,
-    )(sent, jnp.asarray(image_table(bands)))
+    )(exchanged(columns), *held, u_table)
+    return lax.cond(flags[0] == 1, lambda kept: kept, every_slot, image)
 
 
 def solution(mesh):

time: 63.6 us -> 61.1 us (0.961)
  blocking collectives: 22.7 us -> 0 us
  waiting for transfers between devices: 9.69 us -> 27.4 us
  starting transfers between devices: 11.9 us -> 15.3 us
  Pallas kernels: 18.8 us -> 17.1 us
  local copies, waits for them, and re-layouts: 0.03 us -> 0.68 us
    all_to_all x1 -> x0, blocking collectives: 22.7 us -> none  [body(): lax.all_to_all(columns, ('tile', 'chan'), split_axis=0, concat_axis=0, ti...]
    all_to_all x0 -> x1, waiting for transfers between devices: none -> 15.6 us  [exchanged(): lax.all_to_all(columns, ('tile', 'chan'), split_axis=0, concat_axis=0, ti...]
    all_to_all x0 -> x1, starting transfers between devices: none -> 3.41 us  [exchanged(): lax.all_to_all(columns, ('tile', 'chan'), split_axis=0, concat_axis=0, ti...]
    pallas_call x2, Pallas kernels: 8.58 us -> 5.95 us  [the longest x1 3.7 us: body(): pl.pallas_call(functools.partial(image_kernel, scale), out_shape=image_sh...]
    pallas_call x1, Pallas kernels: 4.58 us -> 6.59 us  [body(): pl.pallas_call(functools.partial(grid_kernel, bands, shared), out_shape=(...]
    all_to_all x1, waiting for transfers between devices: 0.01 us -> 1.86 us  [body(): lax.all_to_all(packed, 'tile', split_axis=0, concat_axis=0, tiled=True)]
    pallas_call x1, Pallas kernels: 3.19 us -> 2.09 us  [body(): pl.pallas_call(functools.partial(own_kernel, bands), out_shape=[jax.Shape...]
    unnamed x14 -> x16, local copies, waits for them, and re-layouts: 0.03 us -> 0.68 us
  transfers between devices with their start and end apart: 4 -> 5, of which waited for: 3 -> 5; matrix products, arithmetic and copies ran while one was open for 0% -> 0% of each run, Pallas kernels for 11% -> 7%
where the time goes in v4:
time: 61.1 us; the launch traced here: 60.7 us
  waiting for transfers between devices  27.4 us (45%)
  Pallas kernels  17.1 us (28%)
  starting transfers between devices  15.3 us (25%)
  local copies, waits for them, and re-layouts  0.68 us (1%)
    all_to_all x1, waiting for transfers between devices, exchanged(): lax.all_to_all(columns, ('tile', 'chan'), split_axis=0, concat_axis=0, ti...  15.6 us
    ppermute x3, waiting for transfers between devices, body(): lax.ppermute(own[turn], 'tile', [(band, band ^ turn) for band in range(ba...  9.9 us
    all_to_all x1, starting transfers between devices, body(): lax.all_to_all(packed, 'tile', split_axis=0, concat_axis=0, tiled=True)  8.32 us
    pallas_call x1, Pallas kernels, body(): pl.pallas_call(functools.partial(grid_kernel, bands, shared), out_shape=(...  6.59 us
    pallas_call x1, Pallas kernels, body(): pl.pallas_call(functools.partial(image_kernel, scale), out_shape=image_sh...  3.7 us
    ppermute x3, starting transfers between devices, body(): lax.ppermute(own[turn], 'tile', [(band, band ^ turn) for band in range(ba...  3.55 us
    all_to_all x1, starting transfers between devices, exchanged(): lax.all_to_all(columns, ('tile', 'chan'), split_axis=0, concat_axis=0, ti...  3.41 us
    pallas_call x1, Pallas kernels, body(): pl.pallas_call(functools.partial(pack_kernel, bands, shared), out_shape=j...  2.51 us
  transfers between devices with their start and end apart: 5, of which 5 were waited for; matrix products, arithmetic and copies ran while one was open for 0% of the time, Pallas kernels for 7%

profile of v4, /device:TPU:0, one launch (start us, length us, event | category | flops | bytes accessed | tf_op | source)
XLA Modules:
  0.0 60.7 jit_solution(10800370196404621636)
XLA Ops:
  0.0 2.5 %shard_map.93 = bf16[160,16,128]{2,1,0:T(8,128)(2,1)} custom-call(s32[32]{0:T(128)} %bitcast.29, s32[32]{0:T(128)} %slot_hbm.3, bf16[16,8192]{1,0:T(8,128)(2,1)} %bitcast.17, bf16[16,8192]{1,0:T(8,128)(2,1)} %bitcast.20, bf16[2,2,8192]{2,1,0:T(2,128)(2,1)} %vis_hbm.3, s32[64,128]{1,0:T(8,128)} %bitcast.23, s32[64,128]{1,0:T(8,128)} %bitcast.26), custom_call_target="tpu_custom_call" | custom-call | tf_op jit(solution)/shard_map/pallas_call | solution.py:466
  2.5 8.3 %all-to-all-start.2 = ((bf16[160,16,128]{2,1,0:T(8,128)(2,1)}), bf16[160,16,128]{2,1,0:T(8,128)(2,1)S(1)}, u32[]{:S(2)}, u32[]{:S(2)}) async-start(bf16[160,16,128]{2,1,0:T(8,128)(2,1)} %shard_map.93), calls=%async_computation.2 | async-start | bytes 1310720 | tf_op jit(solution)/shard_map/all_to_all | solution.py:474
  10.9 2.1 %shard_map.94 = (bf16[64,1024]{1,0:T(8,128)(2,1)S(1)}, bf16[64,1024]{1,0:T(8,128)(2,1)S(1)}, bf16[64,1024]{1,0:T(8,128)(2,1)S(1)}, bf16[64,1024]{1,0:T(8,128)(2,1)S(1)}) custom-call(s32[32]{0:T(128)} %bitcast.30, s32[32]{0:T(128)} %slot_hbm.3, bf16[16,8192]{1,0:T(8,128)(2,1)} %bitcast.18, bf16[16,8192]{1,0:T(8,128)(2,1)} %bitcast.21, ...), custom_call_target="tpu_custom_call" | custom-call | flops 1000000000 | bytes 2000000 | tf_op jit(solution)/shard_map/pallas_call | solution.py:478
  13.0 2.0 %collective-permute-start = (bf16[64,1024]{1,0:T(8,128)(2,1)S(1)}, bf16[64,1024]{1,0:T(8,128)(2,1)S(1)}, u32[]{:S(2)}, u32[]{:S(2)}) collective-permute-start(bf16[64,1024]{1,0:T(8,128)(2,1)S(1)} %get-tuple-element.48), channel_id=1, source_target_pairs={{0,2},{2,0},{4,6},{6,4},{8,10},{10,8},{12,14},{14,12},{16,18},{18,... | collective-permute-start | bytes 393224 | tf_op jit(solution)/shard_map/ppermute | solution.py:490
  15.0 1.5 %collective-permute-start.1 = (bf16[64,1024]{1,0:T(8,128)(2,1)S(1)}, bf16[64,1024]{1,0:T(8,128)(2,1)S(1)}, u32[]{:S(2)}, u32[]{:S(2)}) collective-permute-start(bf16[64,1024]{1,0:T(8,128)(2,1)S(1)} %get-tuple-element.49), channel_id=1, source_target_pairs={{0,4},{2,6},{4,0},{6,2},{8,12},{10,14},{12,8},{14,10},{16,20},{18,... | collective-permute-start | bytes 393224 | tf_op jit(solution)/shard_map/ppermute | solution.py:490
  16.4 0.1 collective-permute-start.2
  16.5 5.3 %collective-permute-done.refs_1_ = bf16[64,1024]{1,0:T(8,128)(2,1)S(1)} collective-permute-done((bf16[64,1024]{1,0:T(8,128)(2,1)S(1)}, bf16[64,1024]{1,0:T(8,128)(2,1)S(1)}, u32[]{:S(2)}, u32[]{:S(2)}) %collective-permute-start) | collective-permute-done | bytes 131104 | tf_op jit(solution)/shard_map/ppermute | solution.py:490
  21.8 2.5 %collective-permute-done.1.refs_2_ = bf16[64,1024]{1,0:T(8,128)(2,1)S(1)} collective-permute-done((bf16[64,1024]{1,0:T(8,128)(2,1)S(1)}, bf16[64,1024]{1,0:T(8,128)(2,1)S(1)}, u32[]{:S(2)}, u32[]{:S(2)}) %collective-permute-start.1) | collective-permute-done | bytes 131104 | tf_op jit(solution)/shard_map/ppermute | solution.py:490
  24.4 2.1 %collective-permute-done.2.refs_3_ = bf16[64,1024]{1,0:T(8,128)(2,1)S(1)} collective-permute-done((bf16[64,1024]{1,0:T(8,128)(2,1)S(1)}, bf16[64,1024]{1,0:T(8,128)(2,1)S(1)}, u32[]{:S(2)}, u32[]{:S(2)}) %collective-permute-start.2) | collective-permute-done | bytes 131104 | tf_op jit(solution)/shard_map/ppermute | solution.py:490
  26.4 1.9 %all-to-all-done.2.got_ref = bf16[160,16,128]{2,1,0:T(8,128)(2,1)S(1)} async-done(((bf16[160,16,128]{2,1,0:T(8,128)(2,1)}), bf16[160,16,128]{2,1,0:T(8,128)(2,1)S(1)}, u32[]{:S(2)}, u32[]{:S(2)}) %all-to-all-start.2) | async-done | bytes 655392 | tf_op jit(solution)/shard_map/all_to_all | solution.py:474
  28.3 6.6 %shard_map.95 = (bf16[32,80,128]{2,1,0:T(8,128)(2,1)}, s32[2]{0:T(128)S(1)}) custom-call(bf16[160,16,128]{2,1,0:T(8,128)(2,1)S(1)} %all-to-all-done.2.got_ref, bf16[64,1024]{1,0:T(8,128)(2,1)S(1)} %get-tuple-element.47.refs_0_, bf16[64,1024]{1,0:T(8,128)(2,1)S(1)} %collective-permute-done.refs_1_, bf16[64,1024]{1,0:T(8,128)(2,1)S(1)} %collective-permute-done.1.refs_2_, ...), custom_call_target="tpu_custom_call" | custom-call | tf_op jit(solution)/shard_map/pallas_call | solution.py:493
  34.9 3.4 %all-to-all-start.3 = ((bf16[32,80,128]{2,1,0:T(8,128)(2,1)}), bf16[32,80,128]{2,1,0:T(8,128)(2,1)S(1)}, u32[]{:S(2)}, u32[]{:S(2)}) async-start(bf16[32,80,128]{2,1,0:T(8,128)(2,1)} %get-tuple-element.52), calls=%async_computation.3 | async-start | bytes 1310720 | tf_op jit(solution)/shard_map/all_to_all | solution.py:506
  38.3 2.3 %shard_map.96 = (bf16[256,1024]{1,0:T(8,128)(2,1)S(1)}, bf16[256,1024]{1,0:T(8,128)(2,1)S(1)}, bf16[256,1024]{1,0:T(8,128)(2,1)S(1)}, bf16[256,1024]{1,0:T(8,128)(2,1)S(1)}, bf16[256,1024]{1,0:T(8,128)(2,1)S(1)}) custom-call(s32[2]{0:T(128)S(1)} %get-tuple-element.51.flags, bf16[4096,1024]{1,0:T(8,128)(2,1)} %constant.8.clone.table_hbm.refs_5_), custom_call_target="tpu_custom_call" | custom-call | bytes 16000000 | tf_op jit(solution)/shard_map/pallas_call | solution.py:549
  40.6 15.6 %all-to-all-done.3 = bf16[32,80,128]{2,1,0:T(8,128)(2,1)S(1)} async-done(((bf16[32,80,128]{2,1,0:T(8,128)(2,1)}), bf16[32,80,128]{2,1,0:T(8,128)(2,1)S(1)}, u32[]{:S(2)}, u32[]{:S(2)}) %all-to-all-start.3) | async-done | bytes 655392 | tf_op jit(solution)/shard_map/all_to_all | solution.py:506
  56.2 0.0 copy-start.6
  56.2 0.0 copy-start.7
  56.2 0.0 copy-start.8
  56.3 3.7 %shard_map.97 = f32[32,1024]{1,0:T(8,128)S(1)} custom-call(bf16[16,2,80,128]{3,2,1,0:T(8,128)(2,1)S(1)} %bitcast.14, bf16[256,1024]{1,0:T(8,128)(2,1)S(1)} %get-tuple-element.53.refs_0_, bf16[256,1024]{1,0:T(8,128)(2,1)S(1)} %get-tuple-element.54.refs_1_, bf16[256,1024]{1,0:T(8,128)(2,1)S(1)} %get-tuple-element.55.refs_2_, ...), custom_call_target="tpu_custom_call" | custom-call | tf_op jit(solution)/shard_map/pallas_call | solution.py:559
  60.0 0.0 copy-done.1
  60.0 0.0 copy-done.2
  60.0 0.0 copy-done.3
  60.0 0.0 copy-done.5
  60.1 0.0 copy-start.4
  60.1 0.6 %copy-done.4 = f32[32,1024]{1,0:T(8,128)} copy-done((f32[32,1024]{1,0:T(8,128)}, f32[32,1024]{1,0:T(8,128)S(1)}, u32[]{:S(2)}) %copy-start.4) | copy-done | bytes 131096
  (8 shorter events, 0.0 us)
Async XLA Ops:
  2.5 25.8 %all-to-all-start.2 = ((bf16[160,16,128]{2,1,0:T(8,128)(2,1)}), bf16[160,16,128]{2,1,0:T(8,128)(2,1)S(1)}, u32[]{:S(2)}, u32[]{:S(2)}) async-start(bf16[160,16,128]{2,1,0:T(8,128)(2,1)} %shard_map.93), calls=%async_computation.2 | async-start | bytes 1310720 | tf_op jit(solution)/shard_map/all_to_all | solution.py:474
  13.0 8.9 %collective-permute-start = (bf16[64,1024]{1,0:T(8,128)(2,1)S(1)}, bf16[64,1024]{1,0:T(8,128)(2,1)S(1)}, u32[]{:S(2)}, u32[]{:S(2)}) collective-permute-start(bf16[64,1024]{1,0:T(8,128)(2,1)S(1)} %get-tuple-element.48), channel_id=1, source_target_pairs={{0,2},{2,0},{4,6},{6,4},{8,10},{10,8},{12,14},{14,12},{16,18},{18,... | collective-permute-start | bytes 393224 | tf_op jit(solution)/shard_map/ppermute | solution.py:490
  15.0 9.4 %collective-permute-start.1 = (bf16[64,1024]{1,0:T(8,128)(2,1)S(1)}, bf16[64,1024]{1,0:T(8,128)(2,1)S(1)}, u32[]{:S(2)}, u32[]{:S(2)}) collective-permute-start(bf16[64,1024]{1,0:T(8,128)(2,1)S(1)} %get-tuple-element.49), channel_id=1, source_target_pairs={{0,4},{2,6},{4,0},{6,2},{8,12},{10,14},{12,8},{14,10},{16,20},{18,... | collective-permute-start | bytes 393224 | tf_op jit(solution)/shard_map/ppermute | solution.py:490
  16.4 10.0 %collective-permute-start.2 = (bf16[64,1024]{1,0:T(8,128)(2,1)S(1)}, bf16[64,1024]{1,0:T(8,128)(2,1)S(1)}, u32[]{:S(2)}, u32[]{:S(2)}) collective-permute-start(bf16[64,1024]{1,0:T(8,128)(2,1)S(1)} %get-tuple-element.50), channel_id=1, source_target_pairs={{0,6},{2,4},{4,2},{6,0},{8,14},{10,12},{12,10},{14,8},{16,22},{18,... | collective-permute-start | bytes 393224 | tf_op jit(solution)/shard_map/ppermute | solution.py:490
  34.9 21.3 %all-to-all-start.3 = ((bf16[32,80,128]{2,1,0:T(8,128)(2,1)}), bf16[32,80,128]{2,1,0:T(8,128)(2,1)S(1)}, u32[]{:S(2)}, u32[]{:S(2)}) async-start(bf16[32,80,128]{2,1,0:T(8,128)(2,1)} %get-tuple-element.52), calls=%async_computation.3 | async-start | bytes 1310720 | tf_op jit(solution)/shard_map/all_to_all | solution.py:506
  56.2 3.8 %copy-start.1 = (bf16[2,8,8192]{2,1,0:T(8,128)(2,1)S(1)}, bf16[2,8,8192]{2,1,0:T(8,128)(2,1)}, u32[]{:S(2)}) copy-start(bf16[2,8,8192]{2,1,0:T(8,128)(2,1)} %param.12) | copy-start | bytes 786436
  56.2 3.8 %copy-start.2 = (bf16[2,8,8192]{2,1,0:T(8,128)(2,1)S(1)}, bf16[2,8,8192]{2,1,0:T(8,128)(2,1)}, u32[]{:S(2)}) copy-start(bf16[2,8,8192]{2,1,0:T(8,128)(2,1)} %param.13) | copy-start | bytes 786436
  56.2 3.8 %copy-start.3 = (bf16[2,2,8192]{2,1,0:T(2,128)(2,1)S(1)}, bf16[2,2,8192]{2,1,0:T(2,128)(2,1)}, u32[]{:S(2)}) copy-start(bf16[2,2,8192]{2,1,0:T(2,128)(2,1)} %vis_hbm.3) | copy-start | bytes 196612
  56.2 3.8 %copy-start.5 = (s32[8192]{0:T(1024)S(1)}, s32[8192]{0:T(1024)}, u32[]{:S(2)}) copy-start(s32[8192]{0:T(1024)} %param.14) | copy-start | bytes 98308
  56.2 3.8 %copy-start.6 = (s32[8192]{0:T(1024)S(1)}, s32[8192]{0:T(1024)}, u32[]{:S(2)}) copy-start(s32[8192]{0:T(1024)} %param.15) | copy-start | bytes 98308
  56.2 3.8 %copy-start.7 = (s32[32,1]{0,1:T(1,128)S(1)}, s32[32,1]{0,1:T(1,128)}, u32[]{:S(2)}) copy-start(s32[32,1]{0,1:T(1,128)} %param.16) | copy-start | bytes 388
  56.2 3.8 %copy-start.8 = (s32[32]{0:T(128)S(1)}, s32[32]{0:T(128)}, u32[]{:S(2)}) copy-start(s32[32]{0:T(128)} %slot_hbm.3) | copy-start | bytes 388
  60.1 0.7 %copy-start.4 = (f32[32,1024]{1,0:T(8,128)}, f32[32,1024]{1,0:T(8,128)S(1)}, u32[]{:S(2)}) copy-start(f32[32,1024]{1,0:T(8,128)S(1)} %get-tuple-element.69) | copy-start | bytes 393220

commit v5 on v4

--- a/solution.py
+++ b/solution.py
@@ -200,8 +200,8 @@
 
 def own_kernel(
     bands,
-    route_hbm, slot_hbm, u_hbm, v_hbm, vis_hbm, uo_hbm, vo_hbm, share_0, share_1, share_2, share_3,
-    route, slot, u_ref, v_ref, vis_ref, uo_ref, vo_ref, count, sems, listed, grid,
+    route_hbm, slot_hbm, u_hbm, v_hbm, vis_hbm, uo_hbm, vo_hbm, table_hbm, share_0, share_1, share_2, share_3,
+    route, slot, u_ref, v_ref, vis_ref, uo_ref, vo_ref, count, sems, listed, grid, table, table_sem,
 ):
     copies = start_all(
         (
@@ -210,6 +210,8 @@
         ),
         sems,
     )
+    table_copy = pltpu.make_async_copy(table_hbm, table, table_sem)
+    table_copy.start()
     grid[...] = jnp.zeros_like(grid)
     clear_counts(count, bands)
     copies[0].wait()
@@ -250,10 +252,25 @@
     lax.fori_loop(0, (filled + 3) // 4, add_blocks, 0)
     me = lax.axis_index("tile") % PEERS
     width = TS // PEERS
-    for turn, share_ref in enumerate((share_0, share_1, share_2, share_3)):
+    shares = (share_0, share_1, share_2, share_3)
+    plain, turned_over = [], []
+    for turn in range(PEERS):
         first = pl.multiple_of((me ^ turn) * width, width)
-        for part in range(2):
-            share_ref[part * width:(part + 1) * width, :] = grid[pl.ds(part * TS + first, width), :].astype(jnp.bfloat16)
+        real, imag = [grid[pl.ds(part * TS + first, width), :].astype(jnp.bfloat16) for part in range(2)]
+        plain += [real, imag]
+        turned_over += [-imag, real]
+    both = jnp.concatenate([jnp.concatenate(plain, axis=0), jnp.concatenate(turned_over, axis=0)], axis=1)
+    rows = IMY // share_0.shape[0]
+    step = 256
+    table_copy.wait()
+    for first in range(0, IMY, step):
+        part = dot_rows(table[first:first + step, :], both).astype(jnp.bfloat16)
+        for row in range(0, step, rows):
+            middle = row + rows // 2
+            for turn, share_ref in enumerate(shares):
+                lanes = slice(2 * width * turn, 2 * width * (turn + 1))
+                pieces = [part[row:middle, lanes], part[middle:row + rows, lanes]]
+                share_ref[(first + row) // rows] = jnp.concatenate(pieces, axis=1)
 
 
 def hold_kernel(flags, table_hbm, *refs):
@@ -283,22 +300,15 @@
     return jnp.concatenate([rounded, jnp.concatenate([-rounded[half:], rounded[:half]], axis=0)], axis=1)
 
 
-def write_columns(grid, table, out_ref, own=None):
+def write_columns(grid, table, out_ref):
     both = turned_parts(grid[...].astype(jnp.bfloat16))
-    if own is not None:
-        both = jnp.concatenate([both, turned_parts(own)], axis=0)
     rows = IMY // out_ref.shape[0]
     step = 256
     for first in range(0, IMY, step):
         part = dot_rows(table[first:first + step, :], both)
         for row in range(0, step, rows):
-            pieces = [part[row:row + rows, :TS], part[row:row + rows, TS:2 * TS]]
-            if own is not None:
-                middle = row + rows // 2
-                pieces.append(jnp.concatenate([part[row:middle, 2 * TS:], part[middle:row + rows, 2 * TS:]], axis=1))
-            out_ref[(first + row) // rows, :rows * 2 + (16 if own is not None else 0), :] = jnp.concatenate(
-                pieces, axis=0
-            ).astype(jnp.bfloat16)
+            pieces = [part[row:row + rows, :TS], part[row:row + rows, TS:]]
+            out_ref[(first + row) // rows, :2 * rows, :] = jnp.concatenate(pieces, axis=0).astype(jnp.bfloat16)
 
 
 def full_grid_kernel(places, got_ref, table_hbm, out_ref, grid, table, sem):
@@ -340,18 +350,17 @@
         return jnp.minimum(least, jnp.where(marks == 0.0, float(MANY), marks)), jnp.maximum(most, marks)
 
     start = (jnp.full((8, TS), float(MANY), jnp.float32), jnp.zeros((8, TS), jnp.float32))
-    least, most = lax.fori_loop(0, bands, add_source, start, unroll=4)
+    least, most = lax.fori_loop(0, bands, add_source, start, unroll=8)
     low, high = least[7, 0].astype(jnp.int32), most[7, 0].astype(jnp.int32)
     flags[0] = ((high == 0) | ((low == high) & (high != MANY))).astype(jnp.int32)
     flags[1] = jnp.where(high == MANY, 0, jnp.maximum(high - 1, 0))
-    own = None
     if shared:
         own = shares[0][...].astype(jnp.float32)
         for share in shares[1:]:
             own += share[...].astype(jnp.float32)
-        own = own.astype(jnp.bfloat16)
+        out_ref[:, out_ref.shape[1] - 16:, :] = own.astype(jnp.bfloat16)
     copy.wait()
-    write_columns(grid, table, out_ref, own)
+    write_columns(grid, table, out_ref)
 
 
 def side_by_side(got_ref, band, group, first, rows):
@@ -477,17 +486,18 @@
     if shared:
         own = pl.pallas_call(
             functools.partial(own_kernel, bands),
-            out_shape=[jax.ShapeDtypeStruct((2 * TS // PEERS, TPD * TS), jnp.bfloat16)] * PEERS,
-            in_specs=[HBM] * 7,
+            out_shape=[jax.ShapeDtypeStruct((bands * groups, 16, TS), jnp.bfloat16)] * PEERS,
+            in_specs=[HBM] * 8,
             out_specs=[VMEM] * PEERS,
             scratch_shapes=raw_scratch + [
-                pltpu.SMEM((NB + 1,), jnp.int32), pltpu.VMEM((2 * TS, TPD * TS), jnp.float32)
+                pltpu.SMEM((NB + 1,), jnp.int32), pltpu.VMEM((2 * TS, TPD * TS), jnp.float32),
+                pltpu.VMEM((IMY, 2 * TPD * TS), jnp.bfloat16), pltpu.SemaphoreType.DMA,
             ],
             compiler_params=PARAMS,
-            cost_estimate=pl.CostEstimate(flops=10 ** 9, bytes_accessed=2 * 10 ** 6, transcendentals=0),
-        )(*operands)
+            cost_estimate=pl.CostEstimate(flops=10 ** 9, bytes_accessed=6 * 10 ** 6, transcendentals=0),
+        )(*operands, v_table)
         summed = [own[0]] + [
-            lax.ppermute(own[turn], "tile", [(band, band ^ turn) for band in range(bands)]) for turn in range(1, PEERS)
+            lax.ppermute(own[turn], "tile", [(band, band ^ turn) for band in range(bands)]) for turn in (3, 1, 2)
         ]
         partial = tuple(summed)
     columns, flags = pl.pallas_call(

time: 61.1 us -> 60.4 us (0.989)
  waiting for transfers between devices: 27.4 us -> 25.9 us
    all_to_all x1, waiting for transfers between devices: 1.86 us -> 0.01 us  [body(): lax.all_to_all(packed, 'tile', split_axis=0, concat_axis=0, tiled=True)]
    pallas_call x1, Pallas kernels: 2.09 us -> 3.84 us  [body(): pl.pallas_call(functools.partial(own_kernel, bands), out_shape=[jax.Shape...]
    pallas_call x1, Pallas kernels: 6.59 us -> 5.15 us  [body(): pl.pallas_call(functools.partial(grid_kernel, bands, shared), out_shape=(...]
  transfers between devices with their start and end apart: 5 -> 5, of which waited for: 5 -> 3; matrix products, arithmetic and copies ran while one was open for 0% -> 0% of each run, Pallas kernels for 7% -> 10%
where the time goes in v5:
time: 60.4 us; the launch traced here: 60.1 us
  waiting for transfers between devices  25.9 us (43%)
  Pallas kernels  17.5 us (29%)
  starting transfers between devices  15.9 us (26%)
  local copies, waits for them, and re-layouts  0.68 us (1%)
    all_to_all x1, waiting for transfers between devices, exchanged(): lax.all_to_all(columns, ('tile', 'chan'), split_axis=0, concat_axis=0, ti...  15.6 us
    ppermute x3, waiting for transfers between devices, body(): lax.ppermute(own[turn], 'tile', [(band, band ^ turn) for band in range(ba...  10.2 us
    all_to_all x1, starting transfers between devices, body(): lax.all_to_all(packed, 'tile', split_axis=0, concat_axis=0, tiled=True)  8.32 us
    pallas_call x1, Pallas kernels, body(): pl.pallas_call(functools.partial(grid_kernel, bands, shared), out_shape=(...  5.15 us
    all_to_all x1, starting transfers between devices, exchanged(): lax.all_to_all(columns, ('tile', 'chan'), split_axis=0, concat_axis=0, ti...  3.97 us
    pallas_call x1, Pallas kernels, body(): pl.pallas_call(functools.partial(own_kernel, bands), out_shape=[jax.Shape...  3.84 us
    pallas_call x1, Pallas kernels, body(): pl.pallas_call(functools.partial(image_kernel, scale), out_shape=image_sh...  3.7 us
    ppermute x3, starting transfers between devices, body(): lax.ppermute(own[turn], 'tile', [(band, band ^ turn) for band in range(ba...  3.55 us
  transfers between devices with their start and end apart: 5, of which 3 were waited for; matrix products, arithmetic and copies ran while one was open for 0% of the time, Pallas kernels for 10%

profile of v5, /device:TPU:0, one launch (start us, length us, event | category | flops | bytes accessed | tf_op | source)
XLA Modules:
  0.0 60.1 jit_solution(15986318129874357209)
XLA Ops:
  0.0 2.5 %shard_map.93 = bf16[160,16,128]{2,1,0:T(8,128)(2,1)} custom-call(s32[32]{0:T(128)} %bitcast.29, s32[32]{0:T(128)} %slot_hbm.3, bf16[16,8192]{1,0:T(8,128)(2,1)} %bitcast.17, bf16[16,8192]{1,0:T(8,128)(2,1)} %bitcast.20, bf16[2,2,8192]{2,1,0:T(2,128)(2,1)} %vis_hbm.3, s32[64,128]{1,0:T(8,128)} %bitcast.23, s32[64,128]{1,0:T(8,128)} %bitcast.26), custom_call_target="tpu_custom_call" | custom-call | tf_op jit(solution)/shard_map/pallas_call | solution.py:475
  2.5 8.3 %all-to-all-start.2 = ((bf16[160,16,128]{2,1,0:T(8,128)(2,1)}), bf16[160,16,128]{2,1,0:T(8,128)(2,1)S(1)}, u32[]{:S(2)}, u32[]{:S(2)}) async-start(bf16[160,16,128]{2,1,0:T(8,128)(2,1)} %shard_map.93), calls=%async_computation.2 | async-start | bytes 1310720 | tf_op jit(solution)/shard_map/all_to_all | solution.py:483
  10.9 3.8 %shard_map.94 = (bf16[32,16,128]{2,1,0:T(8,128)(2,1)S(1)}, bf16[32,16,128]{2,1,0:T(8,128)(2,1)S(1)}, bf16[32,16,128]{2,1,0:T(8,128)(2,1)S(1)}, bf16[32,16,128]{2,1,0:T(8,128)(2,1)S(1)}) custom-call(s32[32]{0:T(128)} %bitcast.30, s32[32]{0:T(128)} %slot_hbm.3, bf16[16,8192]{1,0:T(8,128)(2,1)} %bitcast.18, bf16[16,8192]{1,0:T(8,128)(2,1)} %bitcast.21, ...), custom_call_target="tpu_custom_call" | custom-call | flops 1000000000 | bytes 6000000 | tf_op jit(solution)/shard_map/pallas_call | solution.py:487
  14.7 2.9 %collective-permute-start = (bf16[32,16,128]{2,1,0:T(8,128)(2,1)S(1)}, bf16[32,16,128]{2,1,0:T(8,128)(2,1)S(1)}, u32[]{:S(2)}, u32[]{:S(2)}) collective-permute-start(bf16[32,16,128]{2,1,0:T(8,128)(2,1)S(1)} %get-tuple-element.48), channel_id=1, source_target_pairs={{0,6},{2,4},{4,2},{6,0},{8,14},{10,12},{12,10},{14,8},{16,22},{18,... | collective-permute-start | bytes 393224 | tf_op jit(solution)/shard_map/ppermute | solution.py:500
  17.6 0.6 collective-permute-start.1
  18.2 0.1 collective-permute-start.2
  18.3 7.1 %collective-permute-done.refs_1_ = bf16[32,16,128]{2,1,0:T(8,128)(2,1)S(1)} collective-permute-done((bf16[32,16,128]{2,1,0:T(8,128)(2,1)S(1)}, bf16[32,16,128]{2,1,0:T(8,128)(2,1)S(1)}, u32[]{:S(2)}, u32[]{:S(2)}) %collective-permute-start) | collective-permute-done | bytes 131104 | tf_op jit(solution)/shard_map/ppermute | solution.py:500
  25.4 3.1 %collective-permute-done.1.refs_2_ = bf16[32,16,128]{2,1,0:T(8,128)(2,1)S(1)} collective-permute-done((bf16[32,16,128]{2,1,0:T(8,128)(2,1)S(1)}, bf16[32,16,128]{2,1,0:T(8,128)(2,1)S(1)}, u32[]{:S(2)}, u32[]{:S(2)}) %collective-permute-start.1) | collective-permute-done | bytes 131104 | tf_op jit(solution)/shard_map/ppermute | solution.py:500
  28.5 0.0 collective-permute-done.2.refs_3_
  28.5 0.0 all-to-all-done.2.got_ref
  28.5 5.2 %shard_map.95 = (bf16[32,80,128]{2,1,0:T(8,128)(2,1)}, s32[2]{0:T(128)S(1)}) custom-call(bf16[160,16,128]{2,1,0:T(8,128)(2,1)S(1)} %all-to-all-done.2.got_ref, bf16[32,16,128]{2,1,0:T(8,128)(2,1)S(1)} %get-tuple-element.47.refs_0_, bf16[32,16,128]{2,1,0:T(8,128)(2,1)S(1)} %collective-permute-done.refs_1_, ...), custom_call_target="tpu_custom_call" | custom-call | tf_op jit(solution)/shard_map/pallas_call | solution.py:503
  33.7 4.0 %all-to-all-start.3 = ((bf16[32,80,128]{2,1,0:T(8,128)(2,1)}), bf16[32,80,128]{2,1,0:T(8,128)(2,1)S(1)}, u32[]{:S(2)}, u32[]{:S(2)}) async-start(bf16[32,80,128]{2,1,0:T(8,128)(2,1)} %get-tuple-element.52), calls=%async_computation.3 | async-start | bytes 1310720 | tf_op jit(solution)/shard_map/all_to_all | solution.py:516
  37.7 2.3 %shard_map.96 = (bf16[256,1024]{1,0:T(8,128)(2,1)S(1)}, bf16[256,1024]{1,0:T(8,128)(2,1)S(1)}, bf16[256,1024]{1,0:T(8,128)(2,1)S(1)}, bf16[256,1024]{1,0:T(8,128)(2,1)S(1)}, bf16[256,1024]{1,0:T(8,128)(2,1)S(1)}) custom-call(s32[2]{0:T(128)S(1)} %get-tuple-element.51.flags, bf16[4096,1024]{1,0:T(8,128)(2,1)} %constant.8.clone.table_hbm.refs_5_), custom_call_target="tpu_custom_call" | custom-call | bytes 16000000 | tf_op jit(solution)/shard_map/pallas_call | solution.py:559
  40.0 15.6 %all-to-all-done.3 = bf16[32,80,128]{2,1,0:T(8,128)(2,1)S(1)} async-done(((bf16[32,80,128]{2,1,0:T(8,128)(2,1)}), bf16[32,80,128]{2,1,0:T(8,128)(2,1)S(1)}, u32[]{:S(2)}, u32[]{:S(2)}) %all-to-all-start.3) | async-done | bytes 655392 | tf_op jit(solution)/shard_map/all_to_all | solution.py:516
  55.6 0.0 copy-start.5
  55.6 0.0 copy-start.7
  55.6 0.0 copy-start.8
  55.6 3.7 %shard_map.97 = f32[32,1024]{1,0:T(8,128)S(1)} custom-call(bf16[16,2,80,128]{3,2,1,0:T(8,128)(2,1)S(1)} %bitcast.14, bf16[256,1024]{1,0:T(8,128)(2,1)S(1)} %get-tuple-element.53.refs_0_, bf16[256,1024]{1,0:T(8,128)(2,1)S(1)} %get-tuple-element.54.refs_1_, bf16[256,1024]{1,0:T(8,128)(2,1)S(1)} %get-tuple-element.55.refs_2_, ...), custom_call_target="tpu_custom_call" | custom-call | tf_op jit(solution)/shard_map/pallas_call | solution.py:569
  59.3 0.0 copy-done.1
  59.3 0.0 copy-done.2
  59.3 0.0 copy-done.3
  59.4 0.0 copy-done.4
  59.4 0.0 copy-start.6
  59.4 0.6 %copy-done.6 = f32[32,1024]{1,0:T(8,128)} copy-done((f32[32,1024]{1,0:T(8,128)}, f32[32,1024]{1,0:T(8,128)S(1)}, u32[]{:S(2)}) %copy-start.6) | copy-done | bytes 131096
  (8 shorter events, 0.0 us)
Async XLA Ops:
  2.5 26.0 %all-to-all-start.2 = ((bf16[160,16,128]{2,1,0:T(8,128)(2,1)}), bf16[160,16,128]{2,1,0:T(8,128)(2,1)S(1)}, u32[]{:S(2)}, u32[]{:S(2)}) async-start(bf16[160,16,128]{2,1,0:T(8,128)(2,1)} %shard_map.93), calls=%async_computation.2 | async-start | bytes 1310720 | tf_op jit(solution)/shard_map/all_to_all | solution.py:483
  14.7 10.7 %collective-permute-start = (bf16[32,16,128]{2,1,0:T(8,128)(2,1)S(1)}, bf16[32,16,128]{2,1,0:T(8,128)(2,1)S(1)}, u32[]{:S(2)}, u32[]{:S(2)}) collective-permute-start(bf16[32,16,128]{2,1,0:T(8,128)(2,1)S(1)} %get-tuple-element.48), channel_id=1, source_target_pairs={{0,6},{2,4},{4,2},{6,0},{8,14},{10,12},{12,10},{14,8},{16,22},{18,... | collective-permute-start | bytes 393224 | tf_op jit(solution)/shard_map/ppermute | solution.py:500
  17.6 10.9 %collective-permute-start.1 = (bf16[32,16,128]{2,1,0:T(8,128)(2,1)S(1)}, bf16[32,16,128]{2,1,0:T(8,128)(2,1)S(1)}, u32[]{:S(2)}, u32[]{:S(2)}) collective-permute-start(bf16[32,16,128]{2,1,0:T(8,128)(2,1)S(1)} %get-tuple-element.49), channel_id=1, source_target_pairs={{0,2},{2,0},{4,6},{6,4},{8,10},{10,8},{12,14},{14,12},{16,18},{18,... | collective-permute-start | bytes 393224 | tf_op jit(solution)/shard_map/ppermute | solution.py:500
  18.2 10.3 %collective-permute-start.2 = (bf16[32,16,128]{2,1,0:T(8,128)(2,1)S(1)}, bf16[32,16,128]{2,1,0:T(8,128)(2,1)S(1)}, u32[]{:S(2)}, u32[]{:S(2)}) collective-permute-start(bf16[32,16,128]{2,1,0:T(8,128)(2,1)S(1)} %get-tuple-element.50), channel_id=1, source_target_pairs={{0,4},{2,6},{4,0},{6,2},{8,12},{10,14},{12,8},{14,10},{16,20},{18,... | collective-permute-start | bytes 393224 | tf_op jit(solution)/shard_map/ppermute | solution.py:500
  33.7 21.9 %all-to-all-start.3 = ((bf16[32,80,128]{2,1,0:T(8,128)(2,1)}), bf16[32,80,128]{2,1,0:T(8,128)(2,1)S(1)}, u32[]{:S(2)}, u32[]{:S(2)}) async-start(bf16[32,80,128]{2,1,0:T(8,128)(2,1)} %get-tuple-element.52), calls=%async_computation.3 | async-start | bytes 1310720 | tf_op jit(solution)/shard_map/all_to_all | solution.py:516
  55.6 3.8 %copy-start.1 = (bf16[2,8,8192]{2,1,0:T(8,128)(2,1)S(1)}, bf16[2,8,8192]{2,1,0:T(8,128)(2,1)}, u32[]{:S(2)}) copy-start(bf16[2,8,8192]{2,1,0:T(8,128)(2,1)} %param.12) | copy-start | bytes 786436
  55.6 3.8 %copy-start.2 = (bf16[2,8,8192]{2,1,0:T(8,128)(2,1)S(1)}, bf16[2,8,8192]{2,1,0:T(8,128)(2,1)}, u32[]{:S(2)}) copy-start(bf16[2,8,8192]{2,1,0:T(8,128)(2,1)} %param.13) | copy-start | bytes 786436
  55.6 3.8 %copy-start.3 = (bf16[2,2,8192]{2,1,0:T(2,128)(2,1)S(1)}, bf16[2,2,8192]{2,1,0:T(2,128)(2,1)}, u32[]{:S(2)}) copy-start(bf16[2,2,8192]{2,1,0:T(2,128)(2,1)} %vis_hbm.3) | copy-start | bytes 196612
  55.6 3.8 %copy-start.4 = (s32[8192]{0:T(1024)S(1)}, s32[8192]{0:T(1024)}, u32[]{:S(2)}) copy-start(s32[8192]{0:T(1024)} %param.14) | copy-start | bytes 98308
  55.6 3.8 %copy-start.5 = (s32[8192]{0:T(1024)S(1)}, s32[8192]{0:T(1024)}, u32[]{:S(2)}) copy-start(s32[8192]{0:T(1024)} %param.15) | copy-start | bytes 98308
  55.6 3.8 %copy-start.7 = (s32[32,1]{0,1:T(1,128)S(1)}, s32[32,1]{0,1:T(1,128)}, u32[]{:S(2)}) copy-start(s32[32,1]{0,1:T(1,128)} %param.16) | copy-start | bytes 388
  55.6 3.8 %copy-start.8 = (s32[32]{0:T(128)S(1)}, s32[32]{0:T(128)}, u32[]{:S(2)}) copy-start(s32[32]{0:T(128)} %slot_hbm.3) | copy-start | bytes 388
  59.4 0.7 %copy-start.6 = (f32[32,1024]{1,0:T(8,128)}, f32[32,1024]{1,0:T(8,128)S(1)}, u32[]{:S(2)}) copy-start(f32[32,1024]{1,0:T(8,128)S(1)} %get-tuple-element.69) | copy-start | bytes 393220

commit v6 on v5

--- a/solution.py
+++ b/solution.py
@@ -44,7 +44,20 @@
     return both.reshape(bands * 2 * TS, IMX)
 
 
-def full_pack_kernel(capacity, route, slot, u_ref, v_ref, vis_ref, uo_ref, vo_ref, out_ref, count):
+def full_pack_kernel(
+    capacity,
+    route_hbm, slot_hbm, u_hbm, v_hbm, vis_hbm, uo_hbm, vo_hbm, out_ref,
+    route, slot, u_ref, v_ref, vis_ref, uo_ref, vo_ref, count, sems,
+):
+    copies = start_all(
+        (
+            (route_hbm, route), (slot_hbm, slot), (u_hbm, u_ref), (v_hbm, v_ref),
+            (vis_hbm, vis_ref), (uo_hbm, uo_ref), (vo_hbm, vo_ref),
+        ),
+        sems,
+    )
+    for copy in copies:
+        copy.wait()
     owners = out_ref.shape[0] // (capacity * TILES)
     out_ref[...] = jnp.zeros_like(out_ref)
 
@@ -539,10 +552,10 @@
         packed = pl.pallas_call(
             functools.partial(full_pack_kernel, capacity),
             out_shape=jax.ShapeDtypeStruct((slots * TILES, 16, TS), jnp.bfloat16),
-            in_specs=[SMEM, SMEM, VMEM, VMEM, VMEM, VMEM, VMEM],
+            in_specs=[HBM] * 7,
             out_specs=VMEM,
-            scratch_shapes=[pltpu.SMEM((bands,), jnp.int32)],
-            compiler_params=PARAMS,
+            scratch_shapes=raw_scratch,
+            compiler_params=pltpu.CompilerParams(vmem_limit_bytes=63 * 1024 * 1024),
         )(*operands)
         got = lax.all_to_all(packed, "tile", split_axis=0, concat_axis=0, tiled=True)
         places = got.reshape(slots, TILES, 16, TS)[:, TILES - 1, 6, 0].astype(jnp.int32)

time: 60.4 us -> 60.2 us (level)
  local copies, waits for them, and re-layouts: 0.68 us -> 0.01 us
    unnamed x16 -> x6, local copies, waits for them, and re-layouts: 0.68 us -> 0.01 us
where the time goes in v6:
time: 60.2 us; the launch traced here: 59.8 us
  waiting for transfers between devices  25.9 us (43%)
  Pallas kernels  17.9 us (30%)
  starting transfers between devices  15.8 us (26%)
    all_to_all x1, waiting for transfers between devices, exchanged(): lax.all_to_all(columns, ('tile', 'chan'), split_axis=0, concat_axis=0, ti...  15.6 us
    ppermute x3, waiting for transfers between devices, body(): lax.ppermute(own[turn], 'tile', [(band, band ^ turn) for band in range(ba...  10.2 us
    all_to_all x1, starting transfers between devices, body(): lax.all_to_all(packed, 'tile', split_axis=0, concat_axis=0, tiled=True)  8.31 us
    pallas_call x1, Pallas kernels, body(): pl.pallas_call(functools.partial(grid_kernel, bands, shared), out_shape=(...  5.15 us
    pallas_call x1, Pallas kernels, body(): pl.pallas_call(functools.partial(image_kernel, scale), out_shape=image_sh...  4.17 us
    all_to_all x1, starting transfers between devices, exchanged(): lax.all_to_all(columns, ('tile', 'chan'), split_axis=0, concat_axis=0, ti...  3.98 us
    pallas_call x1, Pallas kernels, body(): pl.pallas_call(functools.partial(own_kernel, bands), out_shape=[jax.Shape...  3.85 us
    ppermute x3, starting transfers between devices, body(): lax.ppermute(own[turn], 'tile', [(band, band ^ turn) for band in range(ba...  3.55 us
  transfers between devices with their start and end apart: 5, of which 3 were waited for; matrix products, arithmetic and copies ran while one was open for 0% of the time, Pallas kernels for 10%

profile of v6, /device:TPU:0, one launch (start us, length us, event | category | flops | bytes accessed | tf_op | source)
XLA Modules:
  0.0 59.8 jit_solution(9246093168140420497)
XLA Ops:
  0.0 2.5 %shard_map.93 = bf16[160,16,128]{2,1,0:T(8,128)(2,1)} custom-call(s32[32]{0:T(128)} %bitcast.29, s32[32]{0:T(128)} %slot_hbm.3, bf16[16,8192]{1,0:T(8,128)(2,1)} %bitcast.17, bf16[16,8192]{1,0:T(8,128)(2,1)} %bitcast.20, bf16[2,2,8192]{2,1,0:T(2,128)(2,1)} %vis_hbm.3, s32[64,128]{1,0:T(8,128)} %bitcast.23, s32[64,128]{1,0:T(8,128)} %bitcast.26), custom_call_target="tpu_custom_call" | custom-call | tf_op jit(solution)/shard_map/pallas_call | solution.py:488
  2.5 8.3 %all-to-all-start.2 = ((bf16[160,16,128]{2,1,0:T(8,128)(2,1)}), bf16[160,16,128]{2,1,0:T(8,128)(2,1)S(1)}, u32[]{:S(2)}, u32[]{:S(2)}) async-start(bf16[160,16,128]{2,1,0:T(8,128)(2,1)} %shard_map.93), calls=%async_computation.2 | async-start | bytes 1310720 | tf_op jit(solution)/shard_map/all_to_all | solution.py:496
  10.8 3.8 %shard_map.94 = (bf16[32,16,128]{2,1,0:T(8,128)(2,1)S(1)}, bf16[32,16,128]{2,1,0:T(8,128)(2,1)S(1)}, bf16[32,16,128]{2,1,0:T(8,128)(2,1)S(1)}, bf16[32,16,128]{2,1,0:T(8,128)(2,1)S(1)}) custom-call(s32[32]{0:T(128)} %bitcast.30, s32[32]{0:T(128)} %slot_hbm.3, bf16[16,8192]{1,0:T(8,128)(2,1)} %bitcast.18, bf16[16,8192]{1,0:T(8,128)(2,1)} %bitcast.21, ...), custom_call_target="tpu_custom_call" | custom-call | flops 1000000000 | bytes 6000000 | tf_op jit(solution)/shard_map/pallas_call | solution.py:500
  14.7 2.9 %collective-permute-start = (bf16[32,16,128]{2,1,0:T(8,128)(2,1)S(1)}, bf16[32,16,128]{2,1,0:T(8,128)(2,1)S(1)}, u32[]{:S(2)}, u32[]{:S(2)}) collective-permute-start(bf16[32,16,128]{2,1,0:T(8,128)(2,1)S(1)} %get-tuple-element.48), channel_id=1, source_target_pairs={{0,6},{2,4},{4,2},{6,0},{8,14},{10,12},{12,10},{14,8},{16,22},{18,... | collective-permute-start | bytes 393224 | tf_op jit(solution)/shard_map/ppermute | solution.py:513
  17.6 0.6 collective-permute-start.1
  18.1 0.1 collective-permute-start.2
  18.2 7.1 %collective-permute-done.refs_1_ = bf16[32,16,128]{2,1,0:T(8,128)(2,1)S(1)} collective-permute-done((bf16[32,16,128]{2,1,0:T(8,128)(2,1)S(1)}, bf16[32,16,128]{2,1,0:T(8,128)(2,1)S(1)}, u32[]{:S(2)}, u32[]{:S(2)}) %collective-permute-start) | collective-permute-done | bytes 131104 | tf_op jit(solution)/shard_map/ppermute | solution.py:513
  25.4 3.1 %collective-permute-done.1.refs_2_ = bf16[32,16,128]{2,1,0:T(8,128)(2,1)S(1)} collective-permute-done((bf16[32,16,128]{2,1,0:T(8,128)(2,1)S(1)}, bf16[32,16,128]{2,1,0:T(8,128)(2,1)S(1)}, u32[]{:S(2)}, u32[]{:S(2)}) %collective-permute-start.1) | collective-permute-done | bytes 131104 | tf_op jit(solution)/shard_map/ppermute | solution.py:513
  28.5 0.0 collective-permute-done.2.refs_3_
  28.5 0.0 all-to-all-done.2.got_ref
  28.5 5.2 %shard_map.95 = (bf16[32,80,128]{2,1,0:T(8,128)(2,1)}, s32[2]{0:T(128)S(1)}) custom-call(bf16[160,16,128]{2,1,0:T(8,128)(2,1)S(1)} %all-to-all-done.2.got_ref, bf16[32,16,128]{2,1,0:T(8,128)(2,1)S(1)} %get-tuple-element.47.refs_0_, bf16[32,16,128]{2,1,0:T(8,128)(2,1)S(1)} %collective-permute-done.refs_1_, ...), custom_call_target="tpu_custom_call" | custom-call | tf_op jit(solution)/shard_map/pallas_call | solution.py:516
  33.7 4.0 %all-to-all-start.3 = ((bf16[32,80,128]{2,1,0:T(8,128)(2,1)}), bf16[32,80,128]{2,1,0:T(8,128)(2,1)S(1)}, u32[]{:S(2)}, u32[]{:S(2)}) async-start(bf16[32,80,128]{2,1,0:T(8,128)(2,1)} %get-tuple-element.52), calls=%async_computation.3 | async-start | bytes 1310720 | tf_op jit(solution)/shard_map/all_to_all | solution.py:529
  37.6 2.3 %shard_map.96 = (bf16[256,1024]{1,0:T(8,128)(2,1)S(1)}, bf16[256,1024]{1,0:T(8,128)(2,1)S(1)}, bf16[256,1024]{1,0:T(8,128)(2,1)S(1)}, bf16[256,1024]{1,0:T(8,128)(2,1)S(1)}, bf16[256,1024]{1,0:T(8,128)(2,1)S(1)}) custom-call(s32[2]{0:T(128)S(1)} %get-tuple-element.51.flags, bf16[4096,1024]{1,0:T(8,128)(2,1)} %constant.8.clone.table_hbm.refs_5_), custom_call_target="tpu_custom_call" | custom-call | bytes 16000000 | tf_op jit(solution)/shard_map/pallas_call | solution.py:572
  39.9 15.6 %all-to-all-done.3 = bf16[32,80,128]{2,1,0:T(8,128)(2,1)S(1)} async-done(((bf16[32,80,128]{2,1,0:T(8,128)(2,1)}), bf16[32,80,128]{2,1,0:T(8,128)(2,1)S(1)}, u32[]{:S(2)}, u32[]{:S(2)}) %all-to-all-start.3) | async-done | bytes 655392 | tf_op jit(solution)/shard_map/all_to_all | solution.py:529
  55.6 0.0 copy-start.1
  55.6 0.0 copy-start.2
  55.6 0.0 copy-start.3
  55.6 4.2 %shard_map.97 = f32[32,1024]{1,0:T(8,128)} custom-call(bf16[16,2,80,128]{3,2,1,0:T(8,128)(2,1)S(1)} %bitcast.14, bf16[256,1024]{1,0:T(8,128)(2,1)S(1)} %get-tuple-element.53.refs_0_, bf16[256,1024]{1,0:T(8,128)(2,1)S(1)} %get-tuple-element.54.refs_1_, bf16[256,1024]{1,0:T(8,128)(2,1)S(1)} %get-tuple-element.55.refs_2_, ...), custom_call_target="tpu_custom_call" | custom-call | tf_op jit(solution)/shard_map/pallas_call | solution.py:582
  59.7 0.0 copy-done.1
  59.8 0.0 copy-done.2
  59.8 0.0 copy-done.3
  (1 shorter events, 0.0 us)
Async XLA Ops:
  2.5 26.0 %all-to-all-start.2 = ((bf16[160,16,128]{2,1,0:T(8,128)(2,1)}), bf16[160,16,128]{2,1,0:T(8,128)(2,1)S(1)}, u32[]{:S(2)}, u32[]{:S(2)}) async-start(bf16[160,16,128]{2,1,0:T(8,128)(2,1)} %shard_map.93), calls=%async_computation.2 | async-start | bytes 1310720 | tf_op jit(solution)/shard_map/all_to_all | solution.py:496
  14.7 10.7 %collective-permute-start = (bf16[32,16,128]{2,1,0:T(8,128)(2,1)S(1)}, bf16[32,16,128]{2,1,0:T(8,128)(2,1)S(1)}, u32[]{:S(2)}, u32[]{:S(2)}) collective-permute-start(bf16[32,16,128]{2,1,0:T(8,128)(2,1)S(1)} %get-tuple-element.48), channel_id=1, source_target_pairs={{0,6},{2,4},{4,2},{6,0},{8,14},{10,12},{12,10},{14,8},{16,22},{18,... | collective-permute-start | bytes 393224 | tf_op jit(solution)/shard_map/ppermute | solution.py:513
  17.6 10.9 %collective-permute-start.1 = (bf16[32,16,128]{2,1,0:T(8,128)(2,1)S(1)}, bf16[32,16,128]{2,1,0:T(8,128)(2,1)S(1)}, u32[]{:S(2)}, u32[]{:S(2)}) collective-permute-start(bf16[32,16,128]{2,1,0:T(8,128)(2,1)S(1)} %get-tuple-element.49), channel_id=1, source_target_pairs={{0,2},{2,0},{4,6},{6,4},{8,10},{10,8},{12,14},{14,12},{16,18},{18,... | collective-permute-start | bytes 393224 | tf_op jit(solution)/shard_map/ppermute | solution.py:513
  18.1 10.3 %collective-permute-start.2 = (bf16[32,16,128]{2,1,0:T(8,128)(2,1)S(1)}, bf16[32,16,128]{2,1,0:T(8,128)(2,1)S(1)}, u32[]{:S(2)}, u32[]{:S(2)}) collective-permute-start(bf16[32,16,128]{2,1,0:T(8,128)(2,1)S(1)} %get-tuple-element.50), channel_id=1, source_target_pairs={{0,4},{2,6},{4,0},{6,2},{8,12},{10,14},{12,8},{14,10},{16,20},{18,... | collective-permute-start | bytes 393224 | tf_op jit(solution)/shard_map/ppermute | solution.py:513
  33.7 21.9 %all-to-all-start.3 = ((bf16[32,80,128]{2,1,0:T(8,128)(2,1)}), bf16[32,80,128]{2,1,0:T(8,128)(2,1)S(1)}, u32[]{:S(2)}, u32[]{:S(2)}) async-start(bf16[32,80,128]{2,1,0:T(8,128)(2,1)} %get-tuple-element.52), calls=%async_computation.3 | async-start | bytes 1310720 | tf_op jit(solution)/shard_map/all_to_all | solution.py:529
  55.6 4.2 %copy-start.1 = (bf16[2,8,8192]{2,1,0:T(8,128)(2,1)S(1)}, bf16[2,8,8192]{2,1,0:T(8,128)(2,1)}, u32[]{:S(2)}) copy-start(bf16[2,8,8192]{2,1,0:T(8,128)(2,1)} %param.12) | copy-start | bytes 786436
  55.6 4.2 %copy-start.2 = (s32[32,1]{0,1:T(1,128)S(1)}, s32[32,1]{0,1:T(1,128)}, u32[]{:S(2)}) copy-start(s32[32,1]{0,1:T(1,128)} %param.16) | copy-start | bytes 388
  55.6 4.2 %copy-start.3 = (s32[32]{0:T(128)S(1)}, s32[32]{0:T(128)}, u32[]{:S(2)}) copy-start(s32[32]{0:T(128)} %slot_hbm.3) | copy-start | bytes 388

commit v7 on v6

--- a/solution.py
+++ b/solution.py
@@ -510,7 +510,7 @@
             cost_estimate=pl.CostEstimate(flops=10 ** 9, bytes_accessed=6 * 10 ** 6, transcendentals=0),
         )(*operands, v_table)
         summed = [own[0]] + [
-            lax.ppermute(own[turn], "tile", [(band, band ^ turn) for band in range(bands)]) for turn in (3, 1, 2)
+            lax.ppermute(own[turn], "tile", [(band, band ^ turn) for band in range(bands)]) for turn in (3, 2, 1)
         ]
         partial = tuple(summed)
     columns, flags = pl.pallas_call(

time: 60.2 us -> 60.1 us (level)
  transfers between devices with their start and end apart: 5 -> 5, of which waited for: 3 -> 4; matrix products, arithmetic and copies ran while one was open for 0% -> 0% of each run, Pallas kernels for 10% -> 10%
where the time goes in v7:
time: 60.1 us; the launch traced here: 59.8 us
  waiting for transfers between devices  25.9 us (43%)
  Pallas kernels  17.9 us (30%)
  starting transfers between devices  15.9 us (26%)
    all_to_all x1, waiting for transfers between devices, exchanged(): lax.all_to_all(columns, ('tile', 'chan'), split_axis=0, concat_axis=0, ti...  15.6 us
    ppermute x3, waiting for transfers between devices, body(): lax.ppermute(own[turn], 'tile', [(band, band ^ turn) for band in range(ba...  10.2 us
    all_to_all x1, starting transfers between devices, body(): lax.all_to_all(packed, 'tile', split_axis=0, concat_axis=0, tiled=True)  8.32 us
    pallas_call x1, Pallas kernels, body(): pl.pallas_call(functools.partial(grid_kernel, bands, shared), out_shape=(...  5.14 us
    pallas_call x1, Pallas kernels, body(): pl.pallas_call(functools.partial(image_kernel, scale), out_shape=image_sh...  4.17 us
    all_to_all x1, starting transfers between devices, exchanged(): lax.all_to_all(columns, ('tile', 'chan'), split_axis=0, concat_axis=0, ti...  3.98 us
    pallas_call x1, Pallas kernels, body(): pl.pallas_call(functools.partial(own_kernel, bands), out_shape=[jax.Shape...  3.85 us
    ppermute x3, starting transfers between devices, body(): lax.ppermute(own[turn], 'tile', [(band, band ^ turn) for band in range(ba...  3.55 us
  transfers between devices with their start and end apart: 5, of which 4 were waited for; matrix products, arithmetic and copies ran while one was open for 0% of the time, Pallas kernels for 10%

profile of v7, /device:TPU:0, one launch (start us, length us, event | category | flops | bytes accessed | tf_op | source)
XLA Modules:
  0.0 59.8 jit_solution(9511917850189106248)
XLA Ops:
  0.0 2.5 %shard_map.93 = bf16[160,16,128]{2,1,0:T(8,128)(2,1)} custom-call(s32[32]{0:T(128)} %bitcast.29, s32[32]{0:T(128)} %slot_hbm.3, bf16[16,8192]{1,0:T(8,128)(2,1)} %bitcast.17, bf16[16,8192]{1,0:T(8,128)(2,1)} %bitcast.20, bf16[2,2,8192]{2,1,0:T(2,128)(2,1)} %vis_hbm.3, s32[64,128]{1,0:T(8,128)} %bitcast.23, s32[64,128]{1,0:T(8,128)} %bitcast.26), custom_call_target="tpu_custom_call" | custom-call | tf_op jit(solution)/shard_map/pallas_call | solution.py:488
  2.5 8.3 %all-to-all-start.2 = ((bf16[160,16,128]{2,1,0:T(8,128)(2,1)}), bf16[160,16,128]{2,1,0:T(8,128)(2,1)S(1)}, u32[]{:S(2)}, u32[]{:S(2)}) async-start(bf16[160,16,128]{2,1,0:T(8,128)(2,1)} %shard_map.93), calls=%async_computation.2 | async-start | bytes 1310720 | tf_op jit(solution)/shard_map/all_to_all | solution.py:496
  10.9 3.8 %shard_map.94 = (bf16[32,16,128]{2,1,0:T(8,128)(2,1)S(1)}, bf16[32,16,128]{2,1,0:T(8,128)(2,1)S(1)}, bf16[32,16,128]{2,1,0:T(8,128)(2,1)S(1)}, bf16[32,16,128]{2,1,0:T(8,128)(2,1)S(1)}) custom-call(s32[32]{0:T(128)} %bitcast.30, s32[32]{0:T(128)} %slot_hbm.3, bf16[16,8192]{1,0:T(8,128)(2,1)} %bitcast.18, bf16[16,8192]{1,0:T(8,128)(2,1)} %bitcast.21, ...), custom_call_target="tpu_custom_call" | custom-call | flops 1000000000 | bytes 6000000 | tf_op jit(solution)/shard_map/pallas_call | solution.py:500
  14.7 2.9 %collective-permute-start = (bf16[32,16,128]{2,1,0:T(8,128)(2,1)S(1)}, bf16[32,16,128]{2,1,0:T(8,128)(2,1)S(1)}, u32[]{:S(2)}, u32[]{:S(2)}) collective-permute-start(bf16[32,16,128]{2,1,0:T(8,128)(2,1)S(1)} %get-tuple-element.48), channel_id=1, source_target_pairs={{0,6},{2,4},{4,2},{6,0},{8,14},{10,12},{12,10},{14,8},{16,22},{18,... | collective-permute-start | bytes 393224 | tf_op jit(solution)/shard_map/ppermute | solution.py:513
  17.6 0.6 collective-permute-start.1
  18.2 0.1 collective-permute-start.2
  18.3 7.1 %collective-permute-done.refs_1_ = bf16[32,16,128]{2,1,0:T(8,128)(2,1)S(1)} collective-permute-done((bf16[32,16,128]{2,1,0:T(8,128)(2,1)S(1)}, bf16[32,16,128]{2,1,0:T(8,128)(2,1)S(1)}, u32[]{:S(2)}, u32[]{:S(2)}) %collective-permute-start) | collective-permute-done | bytes 131104 | tf_op jit(solution)/shard_map/ppermute | solution.py:513
  25.4 0.7 %collective-permute-done.1.refs_2_ = bf16[32,16,128]{2,1,0:T(8,128)(2,1)S(1)} collective-permute-done((bf16[32,16,128]{2,1,0:T(8,128)(2,1)S(1)}, bf16[32,16,128]{2,1,0:T(8,128)(2,1)S(1)}, u32[]{:S(2)}, u32[]{:S(2)}) %collective-permute-start.1) | collective-permute-done | bytes 131104 | tf_op jit(solution)/shard_map/ppermute | solution.py:513
  26.1 2.4 %collective-permute-done.2.refs_3_ = bf16[32,16,128]{2,1,0:T(8,128)(2,1)S(1)} collective-permute-done((bf16[32,16,128]{2,1,0:T(8,128)(2,1)S(1)}, bf16[32,16,128]{2,1,0:T(8,128)(2,1)S(1)}, u32[]{:S(2)}, u32[]{:S(2)}) %collective-permute-start.2) | collective-permute-done | bytes 131104 | tf_op jit(solution)/shard_map/ppermute | solution.py:513
  28.5 0.0 all-to-all-done.2.got_ref
  28.5 5.1 %shard_map.95 = (bf16[32,80,128]{2,1,0:T(8,128)(2,1)}, s32[2]{0:T(128)S(1)}) custom-call(bf16[160,16,128]{2,1,0:T(8,128)(2,1)S(1)} %all-to-all-done.2.got_ref, bf16[32,16,128]{2,1,0:T(8,128)(2,1)S(1)} %get-tuple-element.47.refs_0_, bf16[32,16,128]{2,1,0:T(8,128)(2,1)S(1)} %collective-permute-done.refs_1_, ...), custom_call_target="tpu_custom_call" | custom-call | tf_op jit(solution)/shard_map/pallas_call | solution.py:516
  33.7 4.0 %all-to-all-start.3 = ((bf16[32,80,128]{2,1,0:T(8,128)(2,1)}), bf16[32,80,128]{2,1,0:T(8,128)(2,1)S(1)}, u32[]{:S(2)}, u32[]{:S(2)}) async-start(bf16[32,80,128]{2,1,0:T(8,128)(2,1)} %get-tuple-element.52), calls=%async_computation.3 | async-start | bytes 1310720 | tf_op jit(solution)/shard_map/all_to_all | solution.py:529
  37.6 2.3 %shard_map.96 = (bf16[256,1024]{1,0:T(8,128)(2,1)S(1)}, bf16[256,1024]{1,0:T(8,128)(2,1)S(1)}, bf16[256,1024]{1,0:T(8,128)(2,1)S(1)}, bf16[256,1024]{1,0:T(8,128)(2,1)S(1)}, bf16[256,1024]{1,0:T(8,128)(2,1)S(1)}) custom-call(s32[2]{0:T(128)S(1)} %get-tuple-element.51.flags, bf16[4096,1024]{1,0:T(8,128)(2,1)} %constant.8.clone.table_hbm.refs_5_), custom_call_target="tpu_custom_call" | custom-call | bytes 16000000 | tf_op jit(solution)/shard_map/pallas_call | solution.py:572
  39.9 15.6 %all-to-all-done.3 = bf16[32,80,128]{2,1,0:T(8,128)(2,1)S(1)} async-done(((bf16[32,80,128]{2,1,0:T(8,128)(2,1)}), bf16[32,80,128]{2,1,0:T(8,128)(2,1)S(1)}, u32[]{:S(2)}, u32[]{:S(2)}) %all-to-all-start.3) | async-done | bytes 655392 | tf_op jit(solution)/shard_map/all_to_all | solution.py:529
  55.6 0.0 copy-start.1
  55.6 0.0 copy-start.2
  55.6 0.0 copy-start.3
  55.6 4.2 %shard_map.97 = f32[32,1024]{1,0:T(8,128)} custom-call(bf16[16,2,80,128]{3,2,1,0:T(8,128)(2,1)S(1)} %bitcast.14, bf16[256,1024]{1,0:T(8,128)(2,1)S(1)} %get-tuple-element.53.refs_0_, bf16[256,1024]{1,0:T(8,128)(2,1)S(1)} %get-tuple-element.54.refs_1_, bf16[256,1024]{1,0:T(8,128)(2,1)S(1)} %get-tuple-element.55.refs_2_, ...), custom_call_target="tpu_custom_call" | custom-call | tf_op jit(solution)/shard_map/pallas_call | solution.py:582
  59.8 0.0 copy-done.1
  59.8 0.0 copy-done.2
  59.8 0.0 copy-done.3
  (1 shorter events, 0.0 us)
Async XLA Ops:
  2.5 26.0 %all-to-all-start.2 = ((bf16[160,16,128]{2,1,0:T(8,128)(2,1)}), bf16[160,16,128]{2,1,0:T(8,128)(2,1)S(1)}, u32[]{:S(2)}, u32[]{:S(2)}) async-start(bf16[160,16,128]{2,1,0:T(8,128)(2,1)} %shard_map.93), calls=%async_computation.2 | async-start | bytes 1310720 | tf_op jit(solution)/shard_map/all_to_all | solution.py:496
  14.7 10.7 %collective-permute-start = (bf16[32,16,128]{2,1,0:T(8,128)(2,1)S(1)}, bf16[32,16,128]{2,1,0:T(8,128)(2,1)S(1)}, u32[]{:S(2)}, u32[]{:S(2)}) collective-permute-start(bf16[32,16,128]{2,1,0:T(8,128)(2,1)S(1)} %get-tuple-element.48), channel_id=1, source_target_pairs={{0,6},{2,4},{4,2},{6,0},{8,14},{10,12},{12,10},{14,8},{16,22},{18,... | collective-permute-start | bytes 393224 | tf_op jit(solution)/shard_map/ppermute | solution.py:513
  17.6 8.5 %collective-permute-start.1 = (bf16[32,16,128]{2,1,0:T(8,128)(2,1)S(1)}, bf16[32,16,128]{2,1,0:T(8,128)(2,1)S(1)}, u32[]{:S(2)}, u32[]{:S(2)}) collective-permute-start(bf16[32,16,128]{2,1,0:T(8,128)(2,1)S(1)} %get-tuple-element.49), channel_id=1, source_target_pairs={{0,4},{2,6},{4,0},{6,2},{8,12},{10,14},{12,8},{14,10},{16,20},{18,... | collective-permute-start | bytes 393224 | tf_op jit(solution)/shard_map/ppermute | solution.py:513
  18.2 10.4 %collective-permute-start.2 = (bf16[32,16,128]{2,1,0:T(8,128)(2,1)S(1)}, bf16[32,16,128]{2,1,0:T(8,128)(2,1)S(1)}, u32[]{:S(2)}, u32[]{:S(2)}) collective-permute-start(bf16[32,16,128]{2,1,0:T(8,128)(2,1)S(1)} %get-tuple-element.50), channel_id=1, source_target_pairs={{0,2},{2,0},{4,6},{6,4},{8,10},{10,8},{12,14},{14,12},{16,18},{18,... | collective-permute-start | bytes 393224 | tf_op jit(solution)/shard_map/ppermute | solution.py:513
  33.7 21.9 %all-to-all-start.3 = ((bf16[32,80,128]{2,1,0:T(8,128)(2,1)}), bf16[32,80,128]{2,1,0:T(8,128)(2,1)S(1)}, u32[]{:S(2)}, u32[]{:S(2)}) async-start(bf16[32,80,128]{2,1,0:T(8,128)(2,1)} %get-tuple-element.52), calls=%async_computation.3 | async-start | bytes 1310720 | tf_op jit(solution)/shard_map/all_to_all | solution.py:529
  55.6 4.2 %copy-start.1 = (bf16[2,8,8192]{2,1,0:T(8,128)(2,1)S(1)}, bf16[2,8,8192]{2,1,0:T(8,128)(2,1)}, u32[]{:S(2)}) copy-start(bf16[2,8,8192]{2,1,0:T(8,128)(2,1)} %param.12) | copy-start | bytes 786436
  55.6 4.2 %copy-start.2 = (s32[32,1]{0,1:T(1,128)S(1)}, s32[32,1]{0,1:T(1,128)}, u32[]{:S(2)}) copy-start(s32[32,1]{0,1:T(1,128)} %param.16) | copy-start | bytes 388
  55.6 4.2 %copy-start.3 = (s32[32]{0:T(128)S(1)}, s32[32]{0:T(128)}, u32[]{:S(2)}) copy-start(s32[32]{0:T(128)} %slot_hbm.3) | copy-start | bytes 388
